TPU v7x, 32 devices: a whole 2x2x4 slice. The times are simulated.
32 devices in a mesh: rack: 4 (over x, core), node: 8 (over z, y).
Axes of the slice: x: 2, y: 2, z: 4, core: 2. Of those that a mesh axis runs over, the one named last changes fastest.
Arguments:
- stored: bfloat16 [640, 8, 4096], P(('rack', 'node')), may hold values from -6 to 6
- coefficients: bfloat16 [64, 10, 8, 8], replicated, may hold values from -0.3 to 0.61
- helper_rack: int32 [64, 10], replicated, may hold values from 0 to 3, as said below
- helper_node: int32 [64, 10], replicated, may hold values from 0 to 7, as said below
- helper_block: int32 [64, 10], replicated, may hold values from 0 to 19, as said below
Outputs:
- rebuilt: float32 [64, 8, 4096], P(('rack', 'node'))
Inputs may be any that keep to these rules, and one draw needn't show every extreme that they name: Repair r is rebuilt on device r // 2, counted rack-major. Its 10 helpers are distinct devices other than that one. With devices counted rack-major as helper_rack * 8 + helper_node, (helper device minus owner device) mod (32) depends only on h and r mod 2. `helper_node`: follows the same rule as helper_rack. `helper_block`: each of a device's 20 stored blocks is read by exactly one pair of repair and helper.
All inputs are finite; a program needn't handle non-finite values.
Results may differ from a plain program's by a relative error of at most 0.0003.
Values sent between devices are 32-bit elements; how exact they have to be, the bound alone decides.
A program may use at most 64 MiB of HBM per device.

v0:
```python
import jax
import jax.numpy as jnp
from jax import lax
from jax.sharding import PartitionSpec as P

HELPERS = 10
REP_DEV = 2


def from_behind(value, axis, steps):
    count = lax.axis_size(axis)
    pairs = [(source, (source + steps) % count) for source in range(count)]
    return lax.ppermute(value, axis, pairs)


def joint_branch(distance):

    def carry_item(single_item):
        if distance == 0:
            return single_item
        return from_behind(single_item, ("rack", "node"), distance)

    return carry_item


def rotate(payload, moves):
    device_count = lax.axis_size(("rack", "node"))
    joint_table = [joint_branch(distance) for distance in range(device_count)]
    outputs = [
        lax.switch(moves[item_index], joint_table, payload[item_index])
        for item_index in range(payload.shape[0])
    ]
    return jnp.stack(outputs)


def on_device(stored, coefficients, helper_rack, helper_node, helper_block):
    node_count = lax.axis_size("node")
    device_count = lax.axis_size(("rack", "node"))
    my_device = lax.axis_index("rack") * node_count + lax.axis_index("node")
    offsets = (helper_rack[:REP_DEV] * node_count + helper_node[:REP_DEV]) % device_count
    owner = (my_device - offsets) % device_count
    position = jnp.arange(REP_DEV, dtype=jnp.int32)[:, None]
    repair_rows = owner * REP_DEV + position
    helper_slot = jnp.arange(HELPERS, dtype=jnp.int32)[None, :]
    local_rows = helper_block[repair_rows, helper_slot]
    coeffs_used = coefficients[repair_rows, helper_slot]
    blocks_used = stored[local_rows]
    contrib = jnp.einsum(
        "shpq,shql->shpl", coeffs_used, blocks_used, preferred_element_type=jnp.float32
    )
    next_offset = jnp.concatenate([offsets[:, 1:], jnp.zeros_like(offsets[:, :1])], 1)
    hop_moves = jnp.transpose((next_offset - offsets) % device_count)
    contrib_hops = jnp.transpose(contrib, (1, 0, 2, 3))

    def advance(partial_value, hop_data):
        term, moves = hop_data
        return (rotate(partial_value + term, moves), None)

    start_sum = jnp.zeros((REP_DEV,) + contrib.shape[2:], jnp.float32)
    rebuilt, unused = lax.scan(advance, start_sum, (contrib_hops, hop_moves))
    return rebuilt


def solution(mesh):
    placed = (P(("rack", "node"), None, None), P(), P(), P(), P())
    return jax.shard_map(
        on_device,
        mesh=mesh,
        in_specs=placed,
        out_specs=P(("rack", "node"), None, None),
        check_vma=False,
    )
```

profile of v0, /device:TPU:0, one launch (start us, length us, event | category | flops | bytes accessed | tf_op | source)
XLA Modules:
  0.0 204.9 jit_solution(4867692572821364984)
XLA Ops:
  8.1 196.1 %while.10 = (s32[]{:T(128)}, f32[2,8,4096]{2,1,0:T(8,128)S(1)}, s32[10,2]{0,1:T(2,128)S(1)}, f32[10,2,8,4096]{3,2,0,1:T(8,128)}, s32[]{:T(128)}, /*index=5*/s32[1,1]{0,1:T(1,128)}, s32[1,1]{0,1:T(1,128)}) while((s32[]{:T(128)}, f32[2,8,4096]{2,1,0:T(8,128)S(1)}, s32[10,2]{0,1:T(2,128)S(1)}, f32[10,2,8,4096]{3,2,0,1:T(8,128)}, s32[]{:T(128)}, ...), condition=%wide.region_65.66_spmd, body=%wide.region_0.65_spmd.sunk | while | flops 131076 | bytes 2883829 | solution.py:60
  10.3 8.6 %conditional.4 = (f32[1,8,4096]{2,1,0:T(8,128)}) conditional(s32[]{:T(128)} %bitcast.214, f32[2,8,4096]{2,1,0:T(8,128)S(1)} %bitcast_add_fusion.2, f32[2,8,4096]{2,1,0:T(8,128)S(1)} %bitcast_add_fusion.2, f32[2,8,4096]{2,1,0:T(8,128)S(1)} %bitcast_add_fusion.2, f32[2,8,4096]{2,1,0:T(8,128)S(1)} %bitcast_add_fusion.2, ...), branch_computations={%region_33.33_spmd, %region_34.34_spmd, %region_35.35_spmd, %regio... | conditional | bytes 786480 | solution.py:30
  10.4 4.5 %collective-permute-start.43 = (f32[8,4096]{1,0:T(8,128)S(1)}, f32[8,4096]{1,0:T(8,128)}, u32[]{:S(2)}, u32[]{:S(2)}) collective-permute-start(f32[8,4096]{1,0:T(8,128)S(1)} %slice_bitcast_fusion.43), channel_id=1, source_target_pairs={{0,13},{1,14},{2,15},{3,16},{4,17},{5,18},{6,19},{7,20},{8,21},{9,... | collective-permute-start | bytes 393224 | tf_op jit(solution)/shard_map/while/body/eval_jaxpr/cond/branch_13_fun/ppermute | solution.py:13
  14.9 4.1 %collective-permute-done.43 = f32[8,4096]{1,0:T(8,128)} collective-permute-done((f32[8,4096]{1,0:T(8,128)S(1)}, f32[8,4096]{1,0:T(8,128)}, u32[]{:S(2)}, u32[]{:S(2)}) %collective-permute-start.43) | collective-permute-done | bytes 131104 | tf_op jit(solution)/shard_map/while/body/eval_jaxpr/cond/branch_13_fun/ppermute | solution.py:13
  19.5 8.1 %conditional.5 = (f32[1,8,4096]{2,1,0:T(8,128)}) conditional(s32[]{:T(128)} %bitcast.215, f32[2,8,4096]{2,1,0:T(8,128)S(1)} %bitcast_add_fusion.2, f32[2,8,4096]{2,1,0:T(8,128)S(1)} %bitcast_add_fusion.2, f32[2,8,4096]{2,1,0:T(8,128)S(1)} %bitcast_add_fusion.2, f32[2,8,4096]{2,1,0:T(8,128)S(1)} %bitcast_add_fusion.2, ...), branch_computations={%region_1.1_spmd, %region_2.2_spmd, %region_3.3_spmd, %region_4.4_... | conditional | bytes 786480 | solution.py:30
  19.6 5.0 %collective-permute-start.17 = (f32[8,4096]{1,0:T(8,128)S(1)}, f32[8,4096]{1,0:T(8,128)}, u32[]{:S(2)}, u32[]{:S(2)}) collective-permute-start(f32[8,4096]{1,0:T(8,128)S(1)} %slice_bitcast_fusion.17), channel_id=1, source_target_pairs={{0,18},{1,19},{2,20},{3,21},{4,22},{5,23},{6,24},{7,25},{8,26},{9,... | collective-permute-start | bytes 393224 | tf_op jit(solution)/shard_map/while/body/eval_jaxpr/cond/branch_18_fun/ppermute | solution.py:13
  24.6 3.0 %collective-permute-done.17 = f32[8,4096]{1,0:T(8,128)} collective-permute-done((f32[8,4096]{1,0:T(8,128)S(1)}, f32[8,4096]{1,0:T(8,128)}, u32[]{:S(2)}, u32[]{:S(2)}) %collective-permute-start.17) | collective-permute-done | bytes 131104 | tf_op jit(solution)/shard_map/while/body/eval_jaxpr/cond/branch_18_fun/ppermute | solution.py:13
  30.9 8.8 %conditional.4 = (f32[1,8,4096]{2,1,0:T(8,128)}) conditional(s32[]{:T(128)} %bitcast.214, f32[2,8,4096]{2,1,0:T(8,128)S(1)} %bitcast_add_fusion.2, f32[2,8,4096]{2,1,0:T(8,128)S(1)} %bitcast_add_fusion.2, f32[2,8,4096]{2,1,0:T(8,128)S(1)} %bitcast_add_fusion.2, f32[2,8,4096]{2,1,0:T(8,128)S(1)} %bitcast_add_fusion.2, ...), branch_computations={%region_33.33_spmd, %region_34.34_spmd, %region_35.35_spmd, %regio... | conditional | bytes 786480 | solution.py:30
  31.0 5.9 %collective-permute-start.47 = (f32[8,4096]{1,0:T(8,128)S(1)}, f32[8,4096]{1,0:T(8,128)}, u32[]{:S(2)}, u32[]{:S(2)}) collective-permute-start(f32[8,4096]{1,0:T(8,128)S(1)} %slice_bitcast_fusion.47), channel_id=1, source_target_pairs={{0,17},{1,18},{2,19},{3,20},{4,21},{5,22},{6,23},{7,24},{8,25},{9,... | collective-permute-start | bytes 393224 | tf_op jit(solution)/shard_map/while/body/eval_jaxpr/cond/branch_17_fun/ppermute | solution.py:13
  36.9 2.8 %collective-permute-done.47 = f32[8,4096]{1,0:T(8,128)} collective-permute-done((f32[8,4096]{1,0:T(8,128)S(1)}, f32[8,4096]{1,0:T(8,128)}, u32[]{:S(2)}, u32[]{:S(2)}) %collective-permute-start.47) | collective-permute-done | bytes 131104 | tf_op jit(solution)/shard_map/while/body/eval_jaxpr/cond/branch_17_fun/ppermute | solution.py:13
  40.3 7.9 %conditional.5 = (f32[1,8,4096]{2,1,0:T(8,128)}) conditional(s32[]{:T(128)} %bitcast.215, f32[2,8,4096]{2,1,0:T(8,128)S(1)} %bitcast_add_fusion.2, f32[2,8,4096]{2,1,0:T(8,128)S(1)} %bitcast_add_fusion.2, f32[2,8,4096]{2,1,0:T(8,128)S(1)} %bitcast_add_fusion.2, f32[2,8,4096]{2,1,0:T(8,128)S(1)} %bitcast_add_fusion.2, ...), branch_computations={%region_1.1_spmd, %region_2.2_spmd, %region_3.3_spmd, %region_4.4_... | conditional | bytes 786480 | solution.py:30
  40.4 7.8 %collective-permute-done.12 = f32[8,4096]{1,0:T(8,128)} collective-permute-done((f32[8,4096]{1,0:T(8,128)S(1)}, f32[8,4096]{1,0:T(8,128)}, u32[]{:S(2)}, u32[]{:S(2)}) %collective-permute-start.12) | collective-permute-done | bytes 131104 | tf_op jit(solution)/shard_map/while/body/eval_jaxpr/cond/branch_13_fun/ppermute | solution.py:13
  51.4 7.8 %conditional.4 = (f32[1,8,4096]{2,1,0:T(8,128)}) conditional(s32[]{:T(128)} %bitcast.214, f32[2,8,4096]{2,1,0:T(8,128)S(1)} %bitcast_add_fusion.2, f32[2,8,4096]{2,1,0:T(8,128)S(1)} %bitcast_add_fusion.2, f32[2,8,4096]{2,1,0:T(8,128)S(1)} %bitcast_add_fusion.2, f32[2,8,4096]{2,1,0:T(8,128)S(1)} %bitcast_add_fusion.2, ...), branch_computations={%region_33.33_spmd, %region_34.34_spmd, %region_35.35_spmd, %regio... | conditional | bytes 786480 | solution.py:30
  51.6 7.6 %collective-permute-done.43 = f32[8,4096]{1,0:T(8,128)} collective-permute-done((f32[8,4096]{1,0:T(8,128)S(1)}, f32[8,4096]{1,0:T(8,128)}, u32[]{:S(2)}, u32[]{:S(2)}) %collective-permute-start.43) | collective-permute-done | bytes 131104 | tf_op jit(solution)/shard_map/while/body/eval_jaxpr/cond/branch_13_fun/ppermute | solution.py:13
  59.7 6.6 %conditional.5 = (f32[1,8,4096]{2,1,0:T(8,128)}) conditional(s32[]{:T(128)} %bitcast.215, f32[2,8,4096]{2,1,0:T(8,128)S(1)} %bitcast_add_fusion.2, f32[2,8,4096]{2,1,0:T(8,128)S(1)} %bitcast_add_fusion.2, f32[2,8,4096]{2,1,0:T(8,128)S(1)} %bitcast_add_fusion.2, f32[2,8,4096]{2,1,0:T(8,128)S(1)} %bitcast_add_fusion.2, ...), branch_computations={%region_1.1_spmd, %region_2.2_spmd, %region_3.3_spmd, %region_4.4_... | conditional | bytes 786480 | solution.py:30
  59.8 3.2 %collective-permute-start.29 = (f32[8,4096]{1,0:T(8,128)S(1)}, f32[8,4096]{1,0:T(8,128)}, u32[]{:S(2)}, u32[]{:S(2)}) collective-permute-start(f32[8,4096]{1,0:T(8,128)S(1)} %slice_bitcast_fusion.29), channel_id=1, source_target_pairs={{0,30},{1,31},{2,0},{3,1},{4,2},{5,3},{6,4},{7,5},{8,6},{9,7},{10,... | collective-permute-start | bytes 393224 | tf_op jit(solution)/shard_map/while/body/eval_jaxpr/cond/branch_30_fun/ppermute | solution.py:13
  63.1 3.3 %collective-permute-done.29 = f32[8,4096]{1,0:T(8,128)} collective-permute-done((f32[8,4096]{1,0:T(8,128)S(1)}, f32[8,4096]{1,0:T(8,128)}, u32[]{:S(2)}, u32[]{:S(2)}) %collective-permute-start.29) | collective-permute-done | bytes 131104 | tf_op jit(solution)/shard_map/while/body/eval_jaxpr/cond/branch_30_fun/ppermute | solution.py:13
  69.7 7.2 %conditional.4 = (f32[1,8,4096]{2,1,0:T(8,128)}) conditional(s32[]{:T(128)} %bitcast.214, f32[2,8,4096]{2,1,0:T(8,128)S(1)} %bitcast_add_fusion.2, f32[2,8,4096]{2,1,0:T(8,128)S(1)} %bitcast_add_fusion.2, f32[2,8,4096]{2,1,0:T(8,128)S(1)} %bitcast_add_fusion.2, f32[2,8,4096]{2,1,0:T(8,128)S(1)} %bitcast_add_fusion.2, ...), branch_computations={%region_33.33_spmd, %region_34.34_spmd, %region_35.35_spmd, %regio... | conditional | bytes 786480 | solution.py:30
  71.8 5.1 %collective-permute-done.44 = f32[8,4096]{1,0:T(8,128)} collective-permute-done((f32[8,4096]{1,0:T(8,128)S(1)}, f32[8,4096]{1,0:T(8,128)}, u32[]{:S(2)}, u32[]{:S(2)}) %collective-permute-start.44) | collective-permute-done | bytes 131104 | tf_op jit(solution)/shard_map/while/body/eval_jaxpr/cond/branch_14_fun/ppermute | solution.py:13
  77.4 6.9 %conditional.5 = (f32[1,8,4096]{2,1,0:T(8,128)}) conditional(s32[]{:T(128)} %bitcast.215, f32[2,8,4096]{2,1,0:T(8,128)S(1)} %bitcast_add_fusion.2, f32[2,8,4096]{2,1,0:T(8,128)S(1)} %bitcast_add_fusion.2, f32[2,8,4096]{2,1,0:T(8,128)S(1)} %bitcast_add_fusion.2, f32[2,8,4096]{2,1,0:T(8,128)S(1)} %bitcast_add_fusion.2, ...), branch_computations={%region_1.1_spmd, %region_2.2_spmd, %region_3.3_spmd, %region_4.4_... | conditional | bytes 786480 | solution.py:30
  77.6 6.8 %collective-permute-done.27 = f32[8,4096]{1,0:T(8,128)} collective-permute-done((f32[8,4096]{1,0:T(8,128)S(1)}, f32[8,4096]{1,0:T(8,128)}, u32[]{:S(2)}, u32[]{:S(2)}) %collective-permute-start.27) | collective-permute-done | bytes 131104 | tf_op jit(solution)/shard_map/while/body/eval_jaxpr/cond/branch_28_fun/ppermute | solution.py:13
  87.6 7.3 %conditional.4 = (f32[1,8,4096]{2,1,0:T(8,128)}) conditional(s32[]{:T(128)} %bitcast.214, f32[2,8,4096]{2,1,0:T(8,128)S(1)} %bitcast_add_fusion.2, f32[2,8,4096]{2,1,0:T(8,128)S(1)} %bitcast_add_fusion.2, f32[2,8,4096]{2,1,0:T(8,128)S(1)} %bitcast_add_fusion.2, f32[2,8,4096]{2,1,0:T(8,128)S(1)} %bitcast_add_fusion.2, ...), branch_computations={%region_33.33_spmd, %region_34.34_spmd, %region_35.35_spmd, %regio... | conditional | bytes 786480 | solution.py:30
  87.7 4.0 %collective-permute-start.49 = (f32[8,4096]{1,0:T(8,128)S(1)}, f32[8,4096]{1,0:T(8,128)}, u32[]{:S(2)}, u32[]{:S(2)}) collective-permute-start(f32[8,4096]{1,0:T(8,128)S(1)} %slice_bitcast_fusion.49), channel_id=1, source_target_pairs={{0,19},{1,20},{2,21},{3,22},{4,23},{5,24},{6,25},{7,26},{8,27},{9,... | collective-permute-start | bytes 393224 | tf_op jit(solution)/shard_map/while/body/eval_jaxpr/cond/branch_19_fun/ppermute | solution.py:13
  91.7 3.2 %collective-permute-done.49 = f32[8,4096]{1,0:T(8,128)} collective-permute-done((f32[8,4096]{1,0:T(8,128)S(1)}, f32[8,4096]{1,0:T(8,128)}, u32[]{:S(2)}, u32[]{:S(2)}) %collective-permute-start.49) | collective-permute-done | bytes 131104 | tf_op jit(solution)/shard_map/while/body/eval_jaxpr/cond/branch_19_fun/ppermute | solution.py:13
  95.5 11.2 %conditional.5 = (f32[1,8,4096]{2,1,0:T(8,128)}) conditional(s32[]{:T(128)} %bitcast.215, f32[2,8,4096]{2,1,0:T(8,128)S(1)} %bitcast_add_fusion.2, f32[2,8,4096]{2,1,0:T(8,128)S(1)} %bitcast_add_fusion.2, f32[2,8,4096]{2,1,0:T(8,128)S(1)} %bitcast_add_fusion.2, f32[2,8,4096]{2,1,0:T(8,128)S(1)} %bitcast_add_fusion.2, ...), branch_computations={%region_1.1_spmd, %region_2.2_spmd, %region_3.3_spmd, %region_4.4_... | conditional | bytes 786480 | solution.py:30
  95.5 8.2 %collective-permute-start.21 = (f32[8,4096]{1,0:T(8,128)S(1)}, f32[8,4096]{1,0:T(8,128)}, u32[]{:S(2)}, u32[]{:S(2)}) collective-permute-start(f32[8,4096]{1,0:T(8,128)S(1)} %slice_bitcast_fusion.21), channel_id=1, source_target_pairs={{0,22},{1,23},{2,24},{3,25},{4,26},{5,27},{6,28},{7,29},{8,30},{9,... | collective-permute-start | bytes 393224 | tf_op jit(solution)/shard_map/while/body/eval_jaxpr/cond/branch_22_fun/ppermute | solution.py:13
  103.7 3.0 %collective-permute-done.21 = f32[8,4096]{1,0:T(8,128)} collective-permute-done((f32[8,4096]{1,0:T(8,128)S(1)}, f32[8,4096]{1,0:T(8,128)}, u32[]{:S(2)}, u32[]{:S(2)}) %collective-permute-start.21) | collective-permute-done | bytes 131104 | tf_op jit(solution)/shard_map/while/body/eval_jaxpr/cond/branch_22_fun/ppermute | solution.py:13
  109.9 4.6 %conditional.4 = (f32[1,8,4096]{2,1,0:T(8,128)}) conditional(s32[]{:T(128)} %bitcast.214, f32[2,8,4096]{2,1,0:T(8,128)S(1)} %bitcast_add_fusion.2, f32[2,8,4096]{2,1,0:T(8,128)S(1)} %bitcast_add_fusion.2, f32[2,8,4096]{2,1,0:T(8,128)S(1)} %bitcast_add_fusion.2, f32[2,8,4096]{2,1,0:T(8,128)S(1)} %bitcast_add_fusion.2, ...), branch_computations={%region_33.33_spmd, %region_34.34_spmd, %region_35.35_spmd, %regio... | conditional | bytes 786480 | solution.py:30
  110.1 4.5 %collective-permute-done.38 = f32[8,4096]{1,0:T(8,128)} collective-permute-done((f32[8,4096]{1,0:T(8,128)S(1)}, f32[8,4096]{1,0:T(8,128)}, u32[]{:S(2)}, u32[]{:S(2)}) %collective-permute-start.38) | collective-permute-done | bytes 131104 | tf_op jit(solution)/shard_map/while/body/eval_jaxpr/cond/branch_8_fun/ppermute | solution.py:13
  115.1 7.9 %conditional.5 = (f32[1,8,4096]{2,1,0:T(8,128)}) conditional(s32[]{:T(128)} %bitcast.215, f32[2,8,4096]{2,1,0:T(8,128)S(1)} %bitcast_add_fusion.2, f32[2,8,4096]{2,1,0:T(8,128)S(1)} %bitcast_add_fusion.2, f32[2,8,4096]{2,1,0:T(8,128)S(1)} %bitcast_add_fusion.2, f32[2,8,4096]{2,1,0:T(8,128)S(1)} %bitcast_add_fusion.2, ...), branch_computations={%region_1.1_spmd, %region_2.2_spmd, %region_3.3_spmd, %region_4.4_... | conditional | bytes 786480 | solution.py:30
  115.3 7.7 %collective-permute-done.24 = f32[8,4096]{1,0:T(8,128)} collective-permute-done((f32[8,4096]{1,0:T(8,128)S(1)}, f32[8,4096]{1,0:T(8,128)}, u32[]{:S(2)}, u32[]{:S(2)}) %collective-permute-start.24) | collective-permute-done | bytes 131104 | tf_op jit(solution)/shard_map/while/body/eval_jaxpr/cond/branch_25_fun/ppermute | solution.py:13
  126.3 7.0 %conditional.4 = (f32[1,8,4096]{2,1,0:T(8,128)}) conditional(s32[]{:T(128)} %bitcast.214, f32[2,8,4096]{2,1,0:T(8,128)S(1)} %bitcast_add_fusion.2, f32[2,8,4096]{2,1,0:T(8,128)S(1)} %bitcast_add_fusion.2, f32[2,8,4096]{2,1,0:T(8,128)S(1)} %bitcast_add_fusion.2, f32[2,8,4096]{2,1,0:T(8,128)S(1)} %bitcast_add_fusion.2, ...), branch_computations={%region_33.33_spmd, %region_34.34_spmd, %region_35.35_spmd, %regio... | conditional | bytes 786480 | solution.py:30
  126.4 6.9 %collective-permute-done.43 = f32[8,4096]{1,0:T(8,128)} collective-permute-done((f32[8,4096]{1,0:T(8,128)S(1)}, f32[8,4096]{1,0:T(8,128)}, u32[]{:S(2)}, u32[]{:S(2)}) %collective-permute-start.43) | collective-permute-done | bytes 131104 | tf_op jit(solution)/shard_map/while/body/eval_jaxpr/cond/branch_13_fun/ppermute | solution.py:13
  133.8 8.3 %conditional.5 = (f32[1,8,4096]{2,1,0:T(8,128)}) conditional(s32[]{:T(128)} %bitcast.215, f32[2,8,4096]{2,1,0:T(8,128)S(1)} %bitcast_add_fusion.2, f32[2,8,4096]{2,1,0:T(8,128)S(1)} %bitcast_add_fusion.2, f32[2,8,4096]{2,1,0:T(8,128)S(1)} %bitcast_add_fusion.2, f32[2,8,4096]{2,1,0:T(8,128)S(1)} %bitcast_add_fusion.2, ...), branch_computations={%region_1.1_spmd, %region_2.2_spmd, %region_3.3_spmd, %region_4.4_... | conditional | bytes 786480 | solution.py:30
  133.9 4.6 %collective-permute-start.30 = (f32[8,4096]{1,0:T(8,128)S(1)}, f32[8,4096]{1,0:T(8,128)}, u32[]{:S(2)}, u32[]{:S(2)}) collective-permute-start(f32[8,4096]{1,0:T(8,128)S(1)} %slice_bitcast_fusion.30), channel_id=1, source_target_pairs={{0,31},{1,0},{2,1},{3,2},{4,3},{5,4},{6,5},{7,6},{8,7},{9,8},{10,9... | collective-permute-start | bytes 393224 | tf_op jit(solution)/shard_map/while/body/eval_jaxpr/cond/branch_31_fun/ppermute | solution.py:13
  138.6 3.6 %collective-permute-done.30 = f32[8,4096]{1,0:T(8,128)} collective-permute-done((f32[8,4096]{1,0:T(8,128)S(1)}, f32[8,4096]{1,0:T(8,128)}, u32[]{:S(2)}, u32[]{:S(2)}) %collective-permute-start.30) | collective-permute-done | bytes 131104 | tf_op jit(solution)/shard_map/while/body/eval_jaxpr/cond/branch_31_fun/ppermute | solution.py:13
  145.4 10.0 %conditional.4 = (f32[1,8,4096]{2,1,0:T(8,128)}) conditional(s32[]{:T(128)} %bitcast.214, f32[2,8,4096]{2,1,0:T(8,128)S(1)} %bitcast_add_fusion.2, f32[2,8,4096]{2,1,0:T(8,128)S(1)} %bitcast_add_fusion.2, f32[2,8,4096]{2,1,0:T(8,128)S(1)} %bitcast_add_fusion.2, f32[2,8,4096]{2,1,0:T(8,128)S(1)} %bitcast_add_fusion.2, ...), branch_computations={%region_33.33_spmd, %region_34.34_spmd, %region_35.35_spmd, %regio... | conditional | bytes 786480 | solution.py:30
  145.5 9.9 %collective-permute-done.57 = f32[8,4096]{1,0:T(8,128)} collective-permute-done((f32[8,4096]{1,0:T(8,128)S(1)}, f32[8,4096]{1,0:T(8,128)}, u32[]{:S(2)}, u32[]{:S(2)}) %collective-permute-start.57) | collective-permute-done | bytes 131104 | tf_op jit(solution)/shard_map/while/body/eval_jaxpr/cond/branch_27_fun/ppermute | solution.py:13
  156.0 8.3 %conditional.5 = (f32[1,8,4096]{2,1,0:T(8,128)}) conditional(s32[]{:T(128)} %bitcast.215, f32[2,8,4096]{2,1,0:T(8,128)S(1)} %bitcast_add_fusion.2, f32[2,8,4096]{2,1,0:T(8,128)S(1)} %bitcast_add_fusion.2, f32[2,8,4096]{2,1,0:T(8,128)S(1)} %bitcast_add_fusion.2, f32[2,8,4096]{2,1,0:T(8,128)S(1)} %bitcast_add_fusion.2, ...), branch_computations={%region_1.1_spmd, %region_2.2_spmd, %region_3.3_spmd, %region_4.4_... | conditional | bytes 786480 | solution.py:30
  156.1 8.2 %collective-permute-done.11 = f32[8,4096]{1,0:T(8,128)} collective-permute-done((f32[8,4096]{1,0:T(8,128)S(1)}, f32[8,4096]{1,0:T(8,128)}, u32[]{:S(2)}, u32[]{:S(2)}) %collective-permute-start.11) | collective-permute-done | bytes 131104 | tf_op jit(solution)/shard_map/while/body/eval_jaxpr/cond/branch_12_fun/ppermute | solution.py:13
  167.5 7.9 %conditional.4 = (f32[1,8,4096]{2,1,0:T(8,128)}) conditional(s32[]{:T(128)} %bitcast.214, f32[2,8,4096]{2,1,0:T(8,128)S(1)} %bitcast_add_fusion.2, f32[2,8,4096]{2,1,0:T(8,128)S(1)} %bitcast_add_fusion.2, f32[2,8,4096]{2,1,0:T(8,128)S(1)} %bitcast_add_fusion.2, f32[2,8,4096]{2,1,0:T(8,128)S(1)} %bitcast_add_fusion.2, ...), branch_computations={%region_33.33_spmd, %region_34.34_spmd, %region_35.35_spmd, %regio... | conditional | bytes 786480 | solution.py:30
  167.7 7.8 %collective-permute-done.55 = f32[8,4096]{1,0:T(8,128)} collective-permute-done((f32[8,4096]{1,0:T(8,128)S(1)}, f32[8,4096]{1,0:T(8,128)}, u32[]{:S(2)}, u32[]{:S(2)}) %collective-permute-start.55) | collective-permute-done | bytes 131104 | tf_op jit(solution)/shard_map/while/body/eval_jaxpr/cond/branch_25_fun/ppermute | solution.py:13
  176.0 8.6 %conditional.5 = (f32[1,8,4096]{2,1,0:T(8,128)}) conditional(s32[]{:T(128)} %bitcast.215, f32[2,8,4096]{2,1,0:T(8,128)S(1)} %bitcast_add_fusion.2, f32[2,8,4096]{2,1,0:T(8,128)S(1)} %bitcast_add_fusion.2, f32[2,8,4096]{2,1,0:T(8,128)S(1)} %bitcast_add_fusion.2, f32[2,8,4096]{2,1,0:T(8,128)S(1)} %bitcast_add_fusion.2, ...), branch_computations={%region_1.1_spmd, %region_2.2_spmd, %region_3.3_spmd, %region_4.4_... | conditional | bytes 786480 | solution.py:30
  176.1 8.4 %collective-permute-done.16 = f32[8,4096]{1,0:T(8,128)} collective-permute-done((f32[8,4096]{1,0:T(8,128)S(1)}, f32[8,4096]{1,0:T(8,128)}, u32[]{:S(2)}, u32[]{:S(2)}) %collective-permute-start.16) | collective-permute-done | bytes 131104 | tf_op jit(solution)/shard_map/while/body/eval_jaxpr/cond/branch_17_fun/ppermute | solution.py:13
  187.8 7.8 %conditional.4 = (f32[1,8,4096]{2,1,0:T(8,128)}) conditional(s32[]{:T(128)} %bitcast.214, f32[2,8,4096]{2,1,0:T(8,128)S(1)} %bitcast_add_fusion.2, f32[2,8,4096]{2,1,0:T(8,128)S(1)} %bitcast_add_fusion.2, f32[2,8,4096]{2,1,0:T(8,128)S(1)} %bitcast_add_fusion.2, f32[2,8,4096]{2,1,0:T(8,128)S(1)} %bitcast_add_fusion.2, ...), branch_computations={%region_33.33_spmd, %region_34.34_spmd, %region_35.35_spmd, %regio... | conditional | bytes 786480 | solution.py:30
  188.0 7.6 %collective-permute-done.47 = f32[8,4096]{1,0:T(8,128)} collective-permute-done((f32[8,4096]{1,0:T(8,128)S(1)}, f32[8,4096]{1,0:T(8,128)}, u32[]{:S(2)}, u32[]{:S(2)}) %collective-permute-start.47) | collective-permute-done | bytes 131104 | tf_op jit(solution)/shard_map/while/body/eval_jaxpr/cond/branch_17_fun/ppermute | solution.py:13
  196.2 7.0 %conditional.5 = (f32[1,8,4096]{2,1,0:T(8,128)}) conditional(s32[]{:T(128)} %bitcast.215, f32[2,8,4096]{2,1,0:T(8,128)S(1)} %bitcast_add_fusion.2, f32[2,8,4096]{2,1,0:T(8,128)S(1)} %bitcast_add_fusion.2, f32[2,8,4096]{2,1,0:T(8,128)S(1)} %bitcast_add_fusion.2, f32[2,8,4096]{2,1,0:T(8,128)S(1)} %bitcast_add_fusion.2, ...), branch_computations={%region_1.1_spmd, %region_2.2_spmd, %region_3.3_spmd, %region_4.4_... | conditional | bytes 786480 | solution.py:30
  196.3 6.9 %collective-permute-done.11 = f32[8,4096]{1,0:T(8,128)} collective-permute-done((f32[8,4096]{1,0:T(8,128)S(1)}, f32[8,4096]{1,0:T(8,128)}, u32[]{:S(2)}, u32[]{:S(2)}) %collective-permute-start.11) | collective-permute-done | bytes 131104 | tf_op jit(solution)/shard_map/while/body/eval_jaxpr/cond/branch_12_fun/ppermute | solution.py:13
  (95 shorter events, 38.1 us)
Async XLA Ops:
  0.0 5.4 %copy-start = (bf16[20,8,4096]{2,1,0:T(8,128)(2,1)S(1)}, bf16[20,8,4096]{2,1,0:T(8,128)(2,1)}, u32[]{:S(2)}) copy-start(bf16[20,8,4096]{2,1,0:T(8,128)(2,1)} %param.71) | copy-start | bytes 3932164
  0.0 4.4 %copy-start.1 = (s32[64,10]{0,1:T(8,128)S(1)}, s32[64,10]{0,1:T(8,128)}, u32[]{:S(2)}) copy-start(s32[64,10]{0,1:T(8,128)} %param.75) | copy-start | bytes 7684
  10.4 8.6 %collective-permute-start.43 = (f32[8,4096]{1,0:T(8,128)S(1)}, f32[8,4096]{1,0:T(8,128)}, u32[]{:S(2)}, u32[]{:S(2)}) collective-permute-start(f32[8,4096]{1,0:T(8,128)S(1)} %slice_bitcast_fusion.43), channel_id=1, source_target_pairs={{0,13},{1,14},{2,15},{3,16},{4,17},{5,18},{6,19},{7,20},{8,21},{9,... | collective-permute-start | bytes 393224 | tf_op jit(solution)/shard_map/while/body/eval_jaxpr/cond/branch_13_fun/ppermute | solution.py:13
  19.6 8.1 %collective-permute-start.17 = (f32[8,4096]{1,0:T(8,128)S(1)}, f32[8,4096]{1,0:T(8,128)}, u32[]{:S(2)}, u32[]{:S(2)}) collective-permute-start(f32[8,4096]{1,0:T(8,128)S(1)} %slice_bitcast_fusion.17), channel_id=1, source_target_pairs={{0,18},{1,19},{2,20},{3,21},{4,22},{5,23},{6,24},{7,25},{8,26},{9,... | collective-permute-start | bytes 393224 | tf_op jit(solution)/shard_map/while/body/eval_jaxpr/cond/branch_18_fun/ppermute | solution.py:13
  31.0 8.7 %collective-permute-start.47 = (f32[8,4096]{1,0:T(8,128)S(1)}, f32[8,4096]{1,0:T(8,128)}, u32[]{:S(2)}, u32[]{:S(2)}) collective-permute-start(f32[8,4096]{1,0:T(8,128)S(1)} %slice_bitcast_fusion.47), channel_id=1, source_target_pairs={{0,17},{1,18},{2,19},{3,20},{4,21},{5,22},{6,23},{7,24},{8,25},{9,... | collective-permute-start | bytes 393224 | tf_op jit(solution)/shard_map/while/body/eval_jaxpr/cond/branch_17_fun/ppermute | solution.py:13
  40.3 7.8 %collective-permute-start.12 = (f32[8,4096]{1,0:T(8,128)S(1)}, f32[8,4096]{1,0:T(8,128)}, u32[]{:S(2)}, u32[]{:S(2)}) collective-permute-start(f32[8,4096]{1,0:T(8,128)S(1)} %slice_bitcast_fusion.12), channel_id=1, source_target_pairs={{0,13},{1,14},{2,15},{3,16},{4,17},{5,18},{6,19},{7,20},{8,21},{9,... | collective-permute-start | bytes 393224 | tf_op jit(solution)/shard_map/while/body/eval_jaxpr/cond/branch_13_fun/ppermute | solution.py:13
  51.5 7.7 %collective-permute-start.43 = (f32[8,4096]{1,0:T(8,128)S(1)}, f32[8,4096]{1,0:T(8,128)}, u32[]{:S(2)}, u32[]{:S(2)}) collective-permute-start(f32[8,4096]{1,0:T(8,128)S(1)} %slice_bitcast_fusion.43), channel_id=1, source_target_pairs={{0,13},{1,14},{2,15},{3,16},{4,17},{5,18},{6,19},{7,20},{8,21},{9,... | collective-permute-start | bytes 393224 | tf_op jit(solution)/shard_map/while/body/eval_jaxpr/cond/branch_13_fun/ppermute | solution.py:13
  59.8 6.6 %collective-permute-start.29 = (f32[8,4096]{1,0:T(8,128)S(1)}, f32[8,4096]{1,0:T(8,128)}, u32[]{:S(2)}, u32[]{:S(2)}) collective-permute-start(f32[8,4096]{1,0:T(8,128)S(1)} %slice_bitcast_fusion.29), channel_id=1, source_target_pairs={{0,30},{1,31},{2,0},{3,1},{4,2},{5,3},{6,4},{7,5},{8,6},{9,7},{10,... | collective-permute-start | bytes 393224 | tf_op jit(solution)/shard_map/while/body/eval_jaxpr/cond/branch_30_fun/ppermute | solution.py:13
  69.7 7.2 %collective-permute-start.44 = (f32[8,4096]{1,0:T(8,128)S(1)}, f32[8,4096]{1,0:T(8,128)}, u32[]{:S(2)}, u32[]{:S(2)}) collective-permute-start(f32[8,4096]{1,0:T(8,128)S(1)} %slice_bitcast_fusion.44), channel_id=1, source_target_pairs={{0,14},{1,15},{2,16},{3,17},{4,18},{5,19},{6,20},{7,21},{8,22},{9,... | collective-permute-start | bytes 393224 | tf_op jit(solution)/shard_map/while/body/eval_jaxpr/cond/branch_14_fun/ppermute | solution.py:13
  77.5 6.8 %collective-permute-start.27 = (f32[8,4096]{1,0:T(8,128)S(1)}, f32[8,4096]{1,0:T(8,128)}, u32[]{:S(2)}, u32[]{:S(2)}) collective-permute-start(f32[8,4096]{1,0:T(8,128)S(1)} %slice_bitcast_fusion.27), channel_id=1, source_target_pairs={{0,28},{1,29},{2,30},{3,31},{4,0},{5,1},{6,2},{7,3},{8,4},{9,5},{1... | collective-permute-start | bytes 393224 | tf_op jit(solution)/shard_map/while/body/eval_jaxpr/cond/branch_28_fun/ppermute | solution.py:13
  87.7 7.2 %collective-permute-start.49 = (f32[8,4096]{1,0:T(8,128)S(1)}, f32[8,4096]{1,0:T(8,128)}, u32[]{:S(2)}, u32[]{:S(2)}) collective-permute-start(f32[8,4096]{1,0:T(8,128)S(1)} %slice_bitcast_fusion.49), channel_id=1, source_target_pairs={{0,19},{1,20},{2,21},{3,22},{4,23},{5,24},{6,25},{7,26},{8,27},{9,... | collective-permute-start | bytes 393224 | tf_op jit(solution)/shard_map/while/body/eval_jaxpr/cond/branch_19_fun/ppermute | solution.py:13
  95.5 11.1 %collective-permute-start.21 = (f32[8,4096]{1,0:T(8,128)S(1)}, f32[8,4096]{1,0:T(8,128)}, u32[]{:S(2)}, u32[]{:S(2)}) collective-permute-start(f32[8,4096]{1,0:T(8,128)S(1)} %slice_bitcast_fusion.21), channel_id=1, source_target_pairs={{0,22},{1,23},{2,24},{3,25},{4,26},{5,27},{6,28},{7,29},{8,30},{9,... | collective-permute-start | bytes 393224 | tf_op jit(solution)/shard_map/while/body/eval_jaxpr/cond/branch_22_fun/ppermute | solution.py:13
  110.0 4.5 %collective-permute-start.38 = (f32[8,4096]{1,0:T(8,128)S(1)}, f32[8,4096]{1,0:T(8,128)}, u32[]{:S(2)}, u32[]{:S(2)}) collective-permute-start(f32[8,4096]{1,0:T(8,128)S(1)} %slice_bitcast_fusion.38), channel_id=1, source_target_pairs={{0,8},{1,9},{2,10},{3,11},{4,12},{5,13},{6,14},{7,15},{8,16},{9,17... | collective-permute-start | bytes 393224 | tf_op jit(solution)/shard_map/while/body/eval_jaxpr/cond/branch_8_fun/ppermute | solution.py:13
  115.2 7.8 %collective-permute-start.24 = (f32[8,4096]{1,0:T(8,128)S(1)}, f32[8,4096]{1,0:T(8,128)}, u32[]{:S(2)}, u32[]{:S(2)}) collective-permute-start(f32[8,4096]{1,0:T(8,128)S(1)} %slice_bitcast_fusion.24), channel_id=1, source_target_pairs={{0,25},{1,26},{2,27},{3,28},{4,29},{5,30},{6,31},{7,0},{8,1},{9,2}... | collective-permute-start | bytes 393224 | tf_op jit(solution)/shard_map/while/body/eval_jaxpr/cond/branch_25_fun/ppermute | solution.py:13
  126.3 6.9 %collective-permute-start.43 = (f32[8,4096]{1,0:T(8,128)S(1)}, f32[8,4096]{1,0:T(8,128)}, u32[]{:S(2)}, u32[]{:S(2)}) collective-permute-start(f32[8,4096]{1,0:T(8,128)S(1)} %slice_bitcast_fusion.43), channel_id=1, source_target_pairs={{0,13},{1,14},{2,15},{3,16},{4,17},{5,18},{6,19},{7,20},{8,21},{9,... | collective-permute-start | bytes 393224 | tf_op jit(solution)/shard_map/while/body/eval_jaxpr/cond/branch_13_fun/ppermute | solution.py:13
  133.9 8.2 %collective-permute-start.30 = (f32[8,4096]{1,0:T(8,128)S(1)}, f32[8,4096]{1,0:T(8,128)}, u32[]{:S(2)}, u32[]{:S(2)}) collective-permute-start(f32[8,4096]{1,0:T(8,128)S(1)} %slice_bitcast_fusion.30), channel_id=1, source_target_pairs={{0,31},{1,0},{2,1},{3,2},{4,3},{5,4},{6,5},{7,6},{8,7},{9,8},{10,9... | collective-permute-start | bytes 393224 | tf_op jit(solution)/shard_map/while/body/eval_jaxpr/cond/branch_31_fun/ppermute | solution.py:13
  145.5 10.0 %collective-permute-start.57 = (f32[8,4096]{1,0:T(8,128)S(1)}, f32[8,4096]{1,0:T(8,128)}, u32[]{:S(2)}, u32[]{:S(2)}) collective-permute-start(f32[8,4096]{1,0:T(8,128)S(1)} %slice_bitcast_fusion.57), channel_id=1, source_target_pairs={{0,27},{1,28},{2,29},{3,30},{4,31},{5,0},{6,1},{7,2},{8,3},{9,4},{... | collective-permute-start | bytes 393224 | tf_op jit(solution)/shard_map/while/body/eval_jaxpr/cond/branch_27_fun/ppermute | solution.py:13
  156.0 8.2 %collective-permute-start.11 = (f32[8,4096]{1,0:T(8,128)S(1)}, f32[8,4096]{1,0:T(8,128)}, u32[]{:S(2)}, u32[]{:S(2)}) collective-permute-start(f32[8,4096]{1,0:T(8,128)S(1)} %slice_bitcast_fusion.11), channel_id=1, source_target_pairs={{0,12},{1,13},{2,14},{3,15},{4,16},{5,17},{6,18},{7,19},{8,20},{9,... | collective-permute-start | bytes 393224 | tf_op jit(solution)/shard_map/while/body/eval_jaxpr/cond/branch_12_fun/ppermute | solution.py:13
  167.6 7.8 %collective-permute-start.55 = (f32[8,4096]{1,0:T(8,128)S(1)}, f32[8,4096]{1,0:T(8,128)}, u32[]{:S(2)}, u32[]{:S(2)}) collective-permute-start(f32[8,4096]{1,0:T(8,128)S(1)} %slice_bitcast_fusion.55), channel_id=1, source_target_pairs={{0,25},{1,26},{2,27},{3,28},{4,29},{5,30},{6,31},{7,0},{8,1},{9,2}... | collective-permute-start | bytes 393224 | tf_op jit(solution)/shard_map/while/body/eval_jaxpr/cond/branch_25_fun/ppermute | solution.py:13
  176.1 8.5 %collective-permute-start.16 = (f32[8,4096]{1,0:T(8,128)S(1)}, f32[8,4096]{1,0:T(8,128)}, u32[]{:S(2)}, u32[]{:S(2)}) collective-permute-start(f32[8,4096]{1,0:T(8,128)S(1)} %slice_bitcast_fusion.16), channel_id=1, source_target_pairs={{0,17},{1,18},{2,19},{3,20},{4,21},{5,22},{6,23},{7,24},{8,25},{9,... | collective-permute-start | bytes 393224 | tf_op jit(solution)/shard_map/while/body/eval_jaxpr/cond/branch_17_fun/ppermute | solution.py:13
  187.9 7.7 %collective-permute-start.47 = (f32[8,4096]{1,0:T(8,128)S(1)}, f32[8,4096]{1,0:T(8,128)}, u32[]{:S(2)}, u32[]{:S(2)}) collective-permute-start(f32[8,4096]{1,0:T(8,128)S(1)} %slice_bitcast_fusion.47), channel_id=1, source_target_pairs={{0,17},{1,18},{2,19},{3,20},{4,21},{5,22},{6,23},{7,24},{8,25},{9,... | collective-permute-start | bytes 393224 | tf_op jit(solution)/shard_map/while/body/eval_jaxpr/cond/branch_17_fun/ppermute | solution.py:13
  196.2 6.9 %collective-permute-start.11 = (f32[8,4096]{1,0:T(8,128)S(1)}, f32[8,4096]{1,0:T(8,128)}, u32[]{:S(2)}, u32[]{:S(2)}) collective-permute-start(f32[8,4096]{1,0:T(8,128)S(1)} %slice_bitcast_fusion.11), channel_id=1, source_target_pairs={{0,12},{1,13},{2,14},{3,15},{4,16},{5,17},{6,18},{7,19},{8,20},{9,... | collective-permute-start | bytes 393224 | tf_op jit(solution)/shard_map/while/body/eval_jaxpr/cond/branch_12_fun/ppermute | solution.py:13
  204.2 0.7 copy-start.2
where the time goes:
time: 202 us; the launch traced here: 205 us
  waiting for transfers between devices  118 us (58%)
  starting transfers between devices  38.5 us (19%)
  other arithmetic  19.8 us (10%)
  local copies, waits for them, and re-layouts  13.4 us (7%)
  loops' own time  13.3 us (7%)
    ppermute x20, waiting for transfers between devices, from_behind(): return lax.ppermute(value, axis, pairs)  118 us
    ppermute x20, starting transfers between devices, from_behind(): return lax.ppermute(value, axis, pairs)  38.5 us
    another operation x1, loops' own time, on_device(): rebuilt, unused = lax.scan(advance, start_sum, (contrib_hops, hop_moves))  12 us
    another operation x10, other arithmetic, rotate(): return jnp.stack(outputs)  9.86 us
    add x10, other arithmetic, advance(): return (rotate(partial_value + term, moves), None)  9.85 us
    slice x10, local copies, waits for them, and re-layouts, rotate(): moves[item_index]  5.74 us
    unnamed x9, local copies, waits for them, and re-layouts  4.25 us
  transfers between devices with their start and end apart: 20, of which 20 were waited for; matrix products, arithmetic and copies ran while one was open for 0% of the time, Pallas kernels for 0%

commit v1 on v0

v1 whole, which is shorter than its diff:
```python
import functools

import jax
import jax.numpy as jnp
from jax import lax
from jax.experimental import pallas as pl
from jax.experimental.pallas import tpu as pltpu
from jax.sharding import PartitionSpec as P

MESH = pl.DeviceIdType.MESH
CORES = 2
CHUNKS = 4


def repair_kernel(
    sizes,
    marks_ref,
    coeffs_ref,
    stored_ref,
    out_ref,
    weights,
    wide,
    fetched,
    first,
    mid_x,
    mid_y,
    last_x,
    last_y,
    ending,
    core_send,
    core_recv,
    one_send,
    one_recv,
    two_send,
    two_recv,
    three_send,
    three_recv,
):
    nx, ny, nz, helpers, hold, planes, own_rows, width = sizes
    rack, node = lax.axis_index("rack"), lax.axis_index("node")
    x, core = lax.div(rack, CORES), lax.rem(rack, CORES)
    z, y = lax.div(node, ny), lax.rem(node, ny)

    def at_core(step):
        return (x * CORES + lax.rem(core + step, CORES), node)

    def to_x(step):
        return lax.rem(x + step, nx)

    def to_y(step):
        return lax.rem(y + step, ny)

    def to_z(step):
        return lax.rem(z + step, nz)

    def at_x(step):
        return (to_x(step) * CORES + core, node)

    def at_y(step):
        return (rack, z * ny + to_y(step))

    def at_z(step):
        return (rack, to_z(step) * ny + y)

    peers = (
        [at_core(1)]
        + [at_x(s) for s in range(1, nx)]
        + [at_y(s) for s in range(1, ny)]
        + [at_z(s) for s in range(1, nz)]
    )
    barrier = pltpu.get_barrier_semaphore()
    for peer in peers:
        pl.semaphore_signal(barrier, inc=1, device_id=peer, device_id_type=MESH)
    pl.semaphore_wait(barrier, len(peers))

    def remote(source, target, send, recv, device):
        return pltpu.make_async_remote_copy(
            src_ref=source,
            dst_ref=target,
            send_sem=send,
            recv_sem=recv,
            device_id=device,
            device_id_type=MESH,
        )

    def lanes(half, chunk):
        return pl.ds((half * CHUNKS + chunk) * width, width)

    def core_copy(half, chunk):
        return remote(
            wide.at[half, chunk],
            fetched.at[half, chunk],
            core_send.at[half, chunk],
            core_recv.at[half, chunk],
            at_core(1),
        )

    for chunk in range(CHUNKS):
        for half in range(2):
            wide[half, chunk] = stored_ref[:, lanes(half, chunk)].astype(jnp.float32)
            core_copy(half, chunk).start()

    blocks = hold * planes
    group = own_rows // nx
    repairs = group // planes
    column = lax.broadcasted_iota(jnp.int32, (group, blocks), 1)
    column_block = lax.div(column, planes)
    spread_row = lax.broadcasted_iota(jnp.int32, (planes, blocks), 0)
    spread_column = lax.broadcasted_iota(jnp.int32, (planes, blocks), 1)
    spread = (lax.rem(spread_column, planes) == spread_row).astype(jnp.bfloat16)
    for gx in range(nx):
        rack_of = gx * CORES + core
        mine = jnp.zeros((group, blocks), jnp.float32)
        theirs = jnp.zeros((group, blocks), jnp.float32)
        marks = marks_ref[pl.ds(rack_of * group, group), :]
        for helper in range(helpers):
            small = coeffs_ref[pl.ds(rack_of * repairs, repairs), helper]
            small = small.astype(jnp.float32).reshape(group, planes)
            tiled = jnp.dot(
                small.astype(jnp.bfloat16), spread, preferred_element_type=jnp.float32
            )
            mark = marks[:, helper : helper + 1]
            mine = jnp.where(mark == column_block, tiled, mine)
            theirs = jnp.where(mark - hold == column_block, tiled, theirs)
        weights[0, gx * group : (gx + 1) * group, :] = mine.astype(jnp.bfloat16)
        weights[1, gx * group : (gx + 1) * group, :] = theirs.astype(jnp.bfloat16)

    def copies_one(half, chunk):
        if half == 0:
            return [
                remote(
                    first.at[half, chunk, to_x(s)],
                    mid_x.at[chunk, s - 1],
                    one_send.at[half, chunk, s - 1],
                    one_recv.at[half, chunk, s - 1],
                    at_x(s),
                )
                for s in range(1, nx)
            ]
        return [
            remote(
                first.at[half, chunk, :, :, to_y(s)],
                mid_y.at[chunk, s - 1],
                one_send.at[half, chunk, s - 1],
                one_recv.at[half, chunk, s - 1],
                at_y(s),
            )
            for s in range(1, ny)
        ]

    def copies_two(half, chunk):
        if half == 0:
            return [
                remote(
                    mid_x.at[chunk, 0, :, to_y(s)],
                    last_x.at[chunk, s - 1],
                    two_send.at[half, chunk, s - 1],
                    two_recv.at[half, chunk, s - 1],
                    at_y(s),
                )
                for s in range(1, ny)
            ]
        return [
            remote(
                mid_y.at[chunk, 0, to_x(s)],
                last_y.at[chunk, s - 1],
                two_send.at[half, chunk, s - 1],
                two_recv.at[half, chunk, s - 1],
                at_x(s),
            )
            for s in range(1, nx)
        ]

    def copies_three(half, chunk):
        last = last_x if half == 0 else last_y
        return [
            remote(
                last.at[chunk, 0, to_z(s)],
                ending.at[half, chunk, s - 1],
                three_send.at[half, chunk, s - 1],
                three_recv.at[half, chunk, s - 1],
                at_z(s),
            )
            for s in range(1, nz)
        ]

    def stage_one(half, chunk):
        core_copy(half, chunk).wait_recv()
        near = stored_ref[:, lanes(half, chunk)]
        far = fetched[half, chunk].astype(jnp.bfloat16)
        total = jnp.dot(weights[0], near, preferred_element_type=jnp.float32)
        total += jnp.dot(weights[1], far, preferred_element_type=jnp.float32)
        first[half, chunk] = total.reshape(first.shape[2:])
        for copy in copies_one(half, chunk):
            copy.start()

    def stage_two(half, chunk):
        copies = copies_one(half, chunk)
        for copy in copies:
            copy.wait_recv()
        mid = mid_x if half == 0 else mid_y
        if half == 0:
            total = first[half, chunk, x]
        else:
            total = first[half, chunk, :, :, y]
        for slot in range(len(copies)):
            total += mid[chunk, slot]
        mid[chunk, 0] = total
        for copy in copies_two(half, chunk):
            copy.start()

    def stage_three(half, chunk):
        copies = copies_two(half, chunk)
        for copy in copies:
            copy.wait_recv()
        last = last_x if half == 0 else last_y
        if half == 0:
            total = mid_x[chunk, 0, :, y]
        else:
            total = mid_y[chunk, 0, x]
        for slot in range(len(copies)):
            total += last[chunk, slot]
        last[chunk, 0] = total
        for copy in copies_three(half, chunk):
            copy.start()

    def stage_four(half, chunk):
        copies = copies_three(half, chunk)
        for copy in copies:
            copy.wait_recv()
        last = last_x if half == 0 else last_y
        total = last[chunk, 0, z]
        for slot in range(len(copies)):
            total += ending[half, chunk, slot]
        out_ref[:, lanes(half, chunk)] = total

    stages = (stage_one, stage_two, stage_three, stage_four)
    for tick in range(CHUNKS + len(stages) - 1):
        for depth, stage in enumerate(stages):
            chunk = tick - depth
            if 0 <= chunk < CHUNKS:
                for half in range(2):
                    stage(half, chunk)

    for chunk in range(CHUNKS):
        for half in range(2):
            core_copy(half, chunk).wait_send()
            for copies in (copies_one, copies_two, copies_three):
                for copy in copies(half, chunk):
                    copy.wait_send()


def solution(mesh):
    racks, nodes = mesh.shape["rack"], mesh.shape["node"]
    nx, ny = racks // CORES, 2
    nz = nodes // ny

    def on_device(stored, coefficients, helper_rack, helper_node, helper_block):
        hold, planes, length = stored.shape
        repairs, helpers = helper_block.shape
        rep_dev = repairs // (racks * nodes)
        out_rows = rep_dev * planes
        own_rows = repairs * planes // CORES
        width = length // (2 * CHUNKS)
        rack, node = lax.axis_index("rack"), lax.axis_index("node")
        other = rack + 1 - 2 * lax.rem(rack, CORES)
        here = helper_node == node
        marks = jnp.where(
            here & (helper_rack == rack),
            helper_block,
            jnp.where(here & (helper_rack == other), helper_block + hold, -1),
        )
        marks = jnp.broadcast_to(marks[:, None, :], (repairs, planes, helpers))
        marks = marks.reshape(repairs * planes, helpers)
        sizes = (nx, ny, nz, helpers, hold, planes, own_rows, width)
        most = max(nx, ny) - 1
        dma = pltpu.SemaphoreType.DMA
        vmem = pl.BlockSpec(memory_space=pltpu.VMEM)
        rebuilt = pl.pallas_call(
            functools.partial(repair_kernel, sizes),
            out_shape=jax.ShapeDtypeStruct((out_rows, length), jnp.float32),
            in_specs=[vmem] * 3,
            out_specs=vmem,
            scratch_shapes=[
                pltpu.VMEM((2, own_rows, hold * planes), jnp.bfloat16),
                pltpu.VMEM((2, CHUNKS, hold * planes, width), jnp.float32),
                pltpu.VMEM((2, CHUNKS, hold * planes, width), jnp.float32),
                pltpu.VMEM((2, CHUNKS, nx, nz, ny, out_rows, width), jnp.float32),
                pltpu.VMEM((CHUNKS, nx - 1, nz, ny, out_rows, width), jnp.float32),
                pltpu.VMEM((CHUNKS, ny - 1, nx, nz, out_rows, width), jnp.float32),
                pltpu.VMEM((CHUNKS, ny - 1, nz, out_rows, width), jnp.float32),
                pltpu.VMEM((CHUNKS, nx - 1, nz, out_rows, width), jnp.float32),
                pltpu.VMEM((2, CHUNKS, nz - 1, out_rows, width), jnp.float32),
                dma((2, CHUNKS)),
                dma((2, CHUNKS)),
                dma((2, CHUNKS, most)),
                dma((2, CHUNKS, most)),
                dma((2, CHUNKS, most)),
                dma((2, CHUNKS, most)),
                dma((2, CHUNKS, nz - 1)),
                dma((2, CHUNKS, nz - 1)),
            ],
            compiler_params=pltpu.CompilerParams(
                collective_id=0,
                has_side_effects=True,
                vmem_limit_bytes=56 * 1024 * 1024,
            ),
        )(marks, coefficients, stored.reshape(hold * planes, length))
        return rebuilt.reshape(rep_dev, planes, length)

    return jax.shard_map(
        on_device,
        mesh=mesh,
        in_specs=(P(("rack", "node"), None, None), P(), P(), P(), P()),
        out_specs=P(("rack", "node"), None, None),
        check_vma=False,
    )
```

time: 202 us -> 62.7 us (0.31); the launches traced: 205 us -> 62.4 us
  waiting for transfers between devices: 118 us -> 0 us
  Pallas kernels: 0 us -> 56.4 us
  starting transfers between devices: 38.5 us -> 0 us
  other arithmetic: 19.8 us -> 0.74 us
  loops' own time: 13.3 us -> 0 us
  local copies, waits for them, and re-layouts: 13.4 us -> 5.33 us
    ppermute x20 -> x0, waiting for transfers between devices: 118 us -> none  [from_behind(): return lax.ppermute(value, axis, pairs)]
    pallas_call x0 -> x1, Pallas kernels: none -> 56.4 us  [on_device(): pl.pallas_call(functools.partial(repair_kernel, sizes), out_shape=jax.Sha...]
    ppermute x20 -> x0, starting transfers between devices: 38.5 us -> none  [from_behind(): return lax.ppermute(value, axis, pairs)]
    another operation x21 -> x0, loops' own time: 13.3 us -> none  [the longest x1 12 us: on_device(): rebuilt, unused = lax.scan(advance, start_sum, (contrib_hops, hop_moves))]
    another operation x10 -> x0, other arithmetic: 9.86 us -> none  [rotate(): return jnp.stack(outputs)]
    add x10 -> x0, other arithmetic: 9.85 us -> none  [advance(): return (rotate(partial_value + term, moves), None)]
    slice x11 -> x0, local copies, waits for them, and re-layouts: 5.81 us -> none  [the longest x10 5.74 us: rotate(): moves[item_index]]
    gather x4 -> x0, local copies, waits for them, and re-layouts: 2.2 us -> none  [the longest x2 0.87 us: on_device(): local_rows = helper_block[repair_rows, helper_slot]]
  transfers between devices with their start and end apart: 20 -> 0, of which waited for: 20 -> 0; matrix products, arithmetic and copies ran while one was open for 0% -> 0% of each run, Pallas kernels for 0% -> 0%
where the time goes in v1:
time: 62.7 us; the launch traced here: 62.4 us
  Pallas kernels  56.4 us (90%)
  local copies, waits for them, and re-layouts  5.33 us (9%)
  other arithmetic  0.74 us (1%)
    pallas_call x1, Pallas kernels, on_device(): pl.pallas_call(functools.partial(repair_kernel, sizes), out_shape=jax.Sha...  56.4 us
    unnamed x2, local copies, waits for them, and re-layouts  4.52 us

profile of v1, /device:TPU:0, one launch (start us, length us, event | category | flops | bytes accessed | tf_op | source)
XLA Modules:
  0.0 62.4 jit_solution(10106762292134586706)
XLA Ops:
  0.0 0.7 %select_select_fusion = s32[64,10]{0,1:T(8,128)S(1)} fusion(s32[64,10]{0,1:T(8,128)} %param.9, s32[64,10]{0,1:T(8,128)} %param.7, s32[64,10]{0,1:T(8,128)} %param.8, s32[]{:T(128)S(6)} %sub.3, s32[]{:T(128)S(6)} %axis_index.25, s32[]{:T(128)S(6)} %axis_index.22), kind=kLoop, calls=%fused_computation.1 | loop fusion | flops 5120 | bytes 10252 | tf_op jit(solution)/shard_map/jit(_where)/select_n | solution.py:268
  0.7 0.1 copy.6
  0.8 0.7 %broadcast_bitcast_fusion.marks_ref = s32[512,10]{1,0:T(8,128)} fusion(s32[64,10]{1,0:T(8,128)S(1)} %copy.6), kind=kLoop, calls=%fused_computation | loop fusion | bytes 23040 | tf_op jit(solution)/shard_map/reshape | solution.py:274
  1.6 2.8 %copy.7.coeffs_ref = bf16[64,10,8,8]{3,2,1,0:T(8,128)(2,1)} copy(bf16[64,10,8,8]{0,3,2,1:T(8,128)(2,1)} %param.6) | data formatting | bytes 163840 | tf_op args[1]
  4.4 56.4 %shard_map.55 = f32[16,4096]{1,0:T(8,128)} custom-call(s32[512,10]{1,0:T(8,128)} %broadcast_bitcast_fusion.marks_ref, bf16[64,10,8,8]{3,2,1,0:T(8,128)(2,1)} %copy.7.coeffs_ref, bf16[160,4096]{1,0:T(8,128)(2,1)} %bitcast.4), custom_call_target="tpu_custom_call" | custom-call | tf_op jit(solution)/shard_map/pallas_call | solution.py:279
  60.8 1.7 %copy.9 = f32[2,8,4096]{2,1,0:T(8,128)} copy(f32[2,8,4096]{2,1,0:T(8,128)} %bitcast.5) | data formatting | bytes 524288

commit v2 on v0

v2 whole, which is shorter than its diff:
```python
import functools

import jax
import jax.numpy as jnp
from jax import lax
from jax.experimental import pallas as pl
from jax.experimental.pallas import tpu as pltpu
from jax.sharding import PartitionSpec as P

MESH = pl.DeviceIdType.MESH
CORES = 2
TILE = 128
AXES = ("x", "z", "y")


def lay_out(length):
    tiles = length // TILE
    side = tiles // 8
    widths = []
    left = (tiles - side) // 2
    while left:
        widths.append(min(2, left))
        left -= widths[-1]
    spare = tiles - 2 * sum(widths)
    groups, start = [], 0
    for number, wide in enumerate(widths):
        tasks, at = [], start
        plan = [("xyz", wide), ("yxz", wide)]
        if spare:
            plan.append((("zxy", "zyx")[number % 2], 1))
            spare -= 1
        for order, count in plan:
            tasks.append((order, at * TILE, count * TILE))
            at += count
        groups.append((start * TILE, (at - start) * TILE, tasks))
        start = at
    return groups


def repair_kernel(
    sizes,
    groups,
    rack_ref,
    node_ref,
    block_ref,
    coeffs_ref,
    stored_ref,
    out_ref,
    weights,
    core_send,
    core_recv,
    task_send,
    task_recv,
    *buffers,
):
    counts, helpers, hold, planes, repairs, per_rack = sizes
    ny = counts["y"]
    tasks = [task for group in groups for task in group[2]]
    wide, fetched = buffers[: len(groups)], buffers[len(groups) : 2 * len(groups)]
    held = buffers[2 * len(groups) :]
    held = [held[4 * t : 4 * t + 4] for t in range(len(tasks))]

    rack, node = lax.axis_index("rack"), lax.axis_index("node")
    core = lax.rem(rack, CORES)
    place = {"x": lax.div(rack, CORES), "z": lax.div(node, ny), "y": lax.rem(node, ny)}

    def moved(axis, step):
        return lax.rem(place[axis] + step, counts[axis])

    def device(axis, step):
        to = dict(place)
        to[axis] = moved(axis, step)
        return (to["x"] * CORES + core, to["z"] * ny + to["y"])

    other_rack = place["x"] * CORES + lax.rem(core + 1, CORES)
    other_core = (other_rack, node)
    peers = [other_core] + [device(a, s) for a in AXES for s in range(1, counts[a])]
    barrier = pltpu.get_barrier_semaphore()
    for peer in peers:
        pl.semaphore_signal(barrier, inc=1, device_id=peer, device_id_type=MESH)
    pl.semaphore_wait(barrier, len(peers))

    def remote(source, target, send, recv, to):
        return pltpu.make_async_remote_copy(
            src_ref=source,
            dst_ref=target,
            send_sem=send,
            recv_sem=recv,
            device_id=to,
            device_id_type=MESH,
        )

    def core_copy(g):
        return remote(wide[g], fetched[g], core_send.at[g], core_recv.at[g], other_core)

    for g, (start, width, _) in enumerate(groups):
        wide[g][...] = stored_ref[:, start : start + width].astype(jnp.float32)
        core_copy(g).start()

    here = node_ref[...] == node
    marks = jnp.where(
        here & (rack_ref[...] == rack),
        block_ref[...],
        jnp.where(here & (rack_ref[...] == other_rack), block_ref[...] + hold, -1),
    )
    own_rows = repairs * planes // CORES
    row = lax.broadcasted_iota(jnp.int32, (own_rows, repairs), 0)
    row_plane, row_repair = lax.rem(row, planes), lax.div(row, planes)
    row_repair = (
        lax.div(row_repair, per_rack) * CORES + core
    ) * per_rack + lax.rem(row_repair, per_rack)
    hits = row_repair == lax.broadcasted_iota(jnp.int32, (own_rows, repairs), 1)
    slot = lax.broadcasted_iota(jnp.int32, (2 * hold, planes, repairs), 0)
    summed = [jnp.zeros((own_rows, hold * planes), jnp.float32)] * 2
    for plane in range(planes):
        spread = jnp.zeros((2 * hold, planes, repairs), jnp.float32)
        for helper in range(helpers):
            values = coeffs_ref[helper, plane].astype(jnp.float32)[None]
            mark = marks[helper : helper + 1, :][None]
            spread = jnp.where(slot == mark, values, spread)
        spread = spread.reshape(2 * hold * planes, repairs).astype(jnp.bfloat16)
        picked = (hits & (row_plane == plane)).astype(jnp.float32).astype(jnp.bfloat16)
        for part in range(2):
            summed[part] += lax.dot_general(
                picked,
                spread[part * hold * planes : (part + 1) * hold * planes],
                (((1,), (1,)), ((), ())),
                preferred_element_type=jnp.float32,
            )
    for part in range(2):
        weights[part] = summed[part].astype(jnp.bfloat16)

    def before(t, stage):
        order = tasks[t][0]
        left = [axis for axis in AXES if axis not in order[:stage]]
        ahead = (slice(None),) * left.index(order[stage])
        if stage == 0:
            return held[t][0], lambda at: ahead + (at,)
        return held[t][stage], lambda at: (0,) + ahead + (at,)

    def copies(t, stage):
        axis = tasks[t][0][stage]
        source, pick = before(t, stage)
        return [
            remote(
                source.at[pick(moved(axis, s))],
                held[t][stage + 1].at[s - 1],
                task_send.at[t, stage, s - 1],
                task_recv.at[t, stage, s - 1],
                device(axis, s),
            )
            for s in range(1, counts[axis])
        ]

    def gathered(t, stage):
        axis = tasks[t][0][stage]
        source, pick = before(t, stage)
        arrived = copies(t, stage)
        for copy in arrived:
            copy.wait_recv()
        total = source[pick(place[axis])]
        for s in range(len(arrived)):
            total += held[t][stage + 1][s]
        return total

    def begin(g):
        start, width, inside = groups[g]
        core_copy(g).wait_recv()
        near = stored_ref[:, start : start + width]
        far = fetched[g][...].astype(jnp.bfloat16)
        total = jnp.dot(weights[0], near, preferred_element_type=jnp.float32)
        total += jnp.dot(weights[1], far, preferred_element_type=jnp.float32)
        for t in members[g]:
            _, at, count = tasks[t]
            piece = total[:, at - start : at - start + count]
            held[t][0][...] = piece.reshape(held[t][0].shape)
            for copy in copies(t, 0):
                copy.start()

    def advance(g, stage):
        for t in members[g]:
            held[t][stage][0] = gathered(t, stage - 1)
            for copy in copies(t, stage):
                copy.start()

    def finish(g):
        for t in members[g]:
            _, at, count = tasks[t]
            out_ref[:, at : at + count] = gathered(t, len(AXES) - 1)

    members, seen = [], 0
    for _, _, inside in groups:
        members.append(range(seen, seen + len(inside)))
        seen += len(inside)
    steps = (
        begin,
        functools.partial(advance, stage=1),
        functools.partial(advance, stage=2),
        finish,
    )
    for tick in range(len(groups) + len(steps) - 1):
        for depth, step in enumerate(steps):
            if 0 <= tick - depth < len(groups):
                step(tick - depth)

    for g in range(len(groups)):
        core_copy(g).wait_send()
        for t in members[g]:
            for stage in range(len(AXES)):
                for copy in copies(t, stage):
                    copy.wait_send()


def solution(mesh):
    racks, nodes = mesh.shape["rack"], mesh.shape["node"]
    counts = {"x": racks // CORES, "y": 2, "z": nodes // 2}

    def on_device(stored, coefficients, helper_rack, helper_node, helper_block):
        hold, planes, length = stored.shape
        repairs, helpers = helper_block.shape
        out_rows = repairs // (racks * nodes) * planes
        groups = lay_out(length)
        tasks = [task for group in groups for task in group[2]]
        sizes = (counts, helpers, hold, planes, repairs, repairs // racks)
        buffers = [
            pltpu.VMEM((hold * planes, width), jnp.float32)
            for _ in range(2)
            for _, width, _ in groups
        ]
        for order, _, width in tasks:
            for stage in range(len(AXES) + 1):
                left = [counts[a] for a in AXES if a not in order[:stage]]
                if stage:
                    left = [counts[order[stage - 1]] - 1] + left
                buffers.append(pltpu.VMEM((*left, out_rows, width), jnp.float32))
        most = max(counts.values()) - 1
        dma = pltpu.SemaphoreType.DMA
        vmem = pl.BlockSpec(memory_space=pltpu.VMEM)
        rebuilt = pl.pallas_call(
            functools.partial(repair_kernel, sizes, groups),
            out_shape=jax.ShapeDtypeStruct((out_rows, length), jnp.float32),
            in_specs=[vmem] * 5,
            out_specs=vmem,
            scratch_shapes=[
                pltpu.VMEM((2, repairs * planes // CORES, hold * planes), jnp.bfloat16),
                dma((len(groups),)),
                dma((len(groups),)),
                dma((len(tasks), len(AXES), most)),
                dma((len(tasks), len(AXES), most)),
                *buffers,
            ],
            compiler_params=pltpu.CompilerParams(
                collective_id=0,
                has_side_effects=True,
                vmem_limit_bytes=56 * 1024 * 1024,
            ),
        )(
            helper_rack.T,
            helper_node.T,
            helper_block.T,
            coefficients.transpose(1, 2, 3, 0),
            stored.reshape(hold * planes, length),
        )
        return rebuilt.reshape(-1, planes, length)

    return jax.shard_map(
        on_device,
        mesh=mesh,
        in_specs=(P(("rack", "node"), None, None), P(), P(), P(), P()),
        out_specs=P(("rack", "node"), None, None),
        check_vma=False,
    )
```

time: 202 us -> 52.7 us (0.26); the launches traced: 205 us -> 52.6 us
  waiting for transfers between devices: 118 us -> 0 us
  Pallas kernels: 0 us -> 50.9 us
  starting transfers between devices: 38.5 us -> 0 us
  other arithmetic: 19.8 us -> 0 us
  loops' own time: 13.3 us -> 0 us
  local copies, waits for them, and re-layouts: 13.4 us -> 1.67 us
    ppermute x20 -> x0, waiting for transfers between devices: 118 us -> none  [from_behind(): return lax.ppermute(value, axis, pairs)]
    pallas_call x0 -> x1, Pallas kernels: none -> 50.9 us  [on_device(): pl.pallas_call(functools.partial(repair_kernel, sizes, groups), out_shape...]
    ppermute x20 -> x0, starting transfers between devices: 38.5 us -> none  [from_behind(): return lax.ppermute(value, axis, pairs)]
    another operation x21 -> x0, loops' own time: 13.3 us -> none  [the longest x1 12 us: on_device(): rebuilt, unused = lax.scan(advance, start_sum, (contrib_hops, hop_moves))]
    another operation x10 -> x0, other arithmetic: 9.86 us -> none  [rotate(): return jnp.stack(outputs)]
    add x10 -> x0, other arithmetic: 9.85 us -> none  [advance(): return (rotate(partial_value + term, moves), None)]
    slice x11 -> x0, local copies, waits for them, and re-layouts: 5.81 us -> none  [the longest x10 5.74 us: rotate(): moves[item_index]]
    unnamed x9 -> x1, local copies, waits for them, and re-layouts: 4.25 us -> 1.67 us
  transfers between devices with their start and end apart: 20 -> 0, of which waited for: 20 -> 0; matrix products, arithmetic and copies ran while one was open for 0% -> 0% of each run, Pallas kernels for 0% -> 0%
where the time goes in v2:
time: 52.7 us; the launch traced here: 52.6 us
  Pallas kernels  50.9 us (97%)
  local copies, waits for them, and re-layouts  1.67 us (3%)
    pallas_call x1, Pallas kernels, on_device(): pl.pallas_call(functools.partial(repair_kernel, sizes, groups), out_shape...  50.9 us
    unnamed x1, local copies, waits for them, and re-layouts  1.67 us

profile of v2, /device:TPU:0, one launch (start us, length us, event | category | flops | bytes accessed | tf_op | source)
XLA Modules:
  0.0 52.6 jit_solution(2803237773110224524)
XLA Ops:
  0.0 50.9 %shard_map.55 = f32[16,4096]{1,0:T(8,128)} custom-call(s32[10,64]{1,0:T(8,128)} %bitcast.9, s32[10,64]{1,0:T(8,128)} %bitcast.10, s32[10,64]{1,0:T(8,128)} %bitcast.11, bf16[10,8,8,64]{3,2,1,0:T(8,128)(2,1)} %bitcast.8, bf16[160,4096]{1,0:T(8,128)(2,1)} %bitcast.6), custom_call_target="tpu_custom_call" | custom-call | tf_op jit(solution)/shard_map/pallas_call | solution.py:239
  50.9 1.7 %copy.7 = f32[2,8,4096]{2,1,0:T(8,128)} copy(f32[2,8,4096]{2,1,0:T(8,128)} %bitcast.7) | data formatting | bytes 524288

commit v3 on v2

--- a/solution.py
+++ b/solution.py
@@ -1,4 +1,5 @@
 import functools
+import math
 
 import jax
 import jax.numpy as jnp
@@ -19,7 +20,7 @@
     widths = []
     left = (tiles - side) // 2
     while left:
-        widths.append(min(2, left))
+        widths.append(2 if left > 2 else 1)
         left -= widths[-1]
     spare = tiles - 2 * sum(widths)
     groups, start = [], 0
@@ -78,7 +79,6 @@
     barrier = pltpu.get_barrier_semaphore()
     for peer in peers:
         pl.semaphore_signal(barrier, inc=1, device_id=peer, device_id_type=MESH)
-    pl.semaphore_wait(barrier, len(peers))
 
     def remote(source, target, send, recv, to):
         return pltpu.make_async_remote_copy(
@@ -95,7 +95,6 @@
 
     for g, (start, width, _) in enumerate(groups):
         wide[g][...] = stored_ref[:, start : start + width].astype(jnp.float32)
-        core_copy(g).start()
 
     here = node_ref[...] == node
     marks = jnp.where(
@@ -113,6 +112,10 @@
     slot = lax.broadcasted_iota(jnp.int32, (2 * hold, planes, repairs), 0)
     summed = [jnp.zeros((own_rows, hold * planes), jnp.float32)] * 2
     for plane in range(planes):
+        if plane == planes // 2:
+            pl.semaphore_wait(barrier, len(peers))
+            for g in range(len(groups)):
+                core_copy(g).start()
         spread = jnp.zeros((2 * hold, planes, repairs), jnp.float32)
         for helper in range(helpers):
             values = coeffs_ref[helper, plane].astype(jnp.float32)[None]
@@ -198,10 +201,11 @@
         functools.partial(advance, stage=2),
         finish,
     )
-    for tick in range(len(groups) + len(steps) - 1):
-        for depth, step in enumerate(steps):
-            if 0 <= tick - depth < len(groups):
-                step(tick - depth)
+    delays = (0, 1, 2, 6)
+    for tick in range(len(groups) + delays[-1]):
+        for delay, step in zip(delays, steps):
+            if 0 <= tick - delay < len(groups):
+                step(tick - delay)
 
     for g in range(len(groups)):
         core_copy(g).wait_send()
@@ -236,10 +240,18 @@
         most = max(counts.values()) - 1
         dma = pltpu.SemaphoreType.DMA
         vmem = pl.BlockSpec(memory_space=pltpu.VMEM)
+        operands = (
+            helper_rack.T,
+            helper_node.T,
+            helper_block.T,
+            coefficients.transpose(1, 2, 3, 0),
+            stored.reshape(hold * planes, length),
+        )
+        buffer_bytes = sum(math.prod(b.shape) * 4 for b in buffers)
         rebuilt = pl.pallas_call(
             functools.partial(repair_kernel, sizes, groups),
             out_shape=jax.ShapeDtypeStruct((out_rows, length), jnp.float32),
-            in_specs=[vmem] * 5,
+            in_specs=[vmem] * len(operands),
             out_specs=vmem,
             scratch_shapes=[
                 pltpu.VMEM((2, repairs * planes // CORES, hold * planes), jnp.bfloat16),
@@ -252,15 +264,9 @@
             compiler_params=pltpu.CompilerParams(
                 collective_id=0,
                 has_side_effects=True,
-                vmem_limit_bytes=56 * 1024 * 1024,
+                vmem_limit_bytes=buffer_bytes + 12 * 1024 * 1024,
             ),
-        )(
-            helper_rack.T,
-            helper_node.T,
-            helper_block.T,
-            coefficients.transpose(1, 2, 3, 0),
-            stored.reshape(hold * planes, length),
-        )
+        )(*operands)
         return rebuilt.reshape(-1, planes, length)
 
     return jax.shard_map(

time: 52.7 us -> 53.7 us (1.019)
  local copies, waits for them, and re-layouts: 1.67 us -> 5.03 us
  Pallas kernels: 50.9 us -> 48.3 us
    unnamed x1 -> x11, local copies, waits for them, and re-layouts: 1.67 us -> 5.03 us
    pallas_call x1, Pallas kernels: 50.9 us -> 48.3 us  [on_device(): pl.pallas_call(functools.partial(repair_kernel, sizes, groups), out_shape...]
where the time goes in v3:
time: 53.7 us; the launch traced here: 53.4 us
  Pallas kernels  48.3 us (90%)
  local copies, waits for them, and re-layouts  5.03 us (9%)
    pallas_call x1, Pallas kernels, on_device(): pl.pallas_call(functools.partial(repair_kernel, sizes, groups), out_shape...  48.3 us
    unnamed x11, local copies, waits for them, and re-layouts  5.03 us

profile of v3, /device:TPU:0, one launch (start us, length us, event | category | flops | bytes accessed | tf_op | source)
XLA Modules:
  0.0 53.4 jit_solution(631563133426584740)
XLA Ops:
  0.0 0.0 copy-start
  0.0 1.3 %copy-done = bf16[20,8,4096]{2,1,0:T(8,128)(2,1)S(1)} copy-done((bf16[20,8,4096]{2,1,0:T(8,128)(2,1)S(1)}, bf16[20,8,4096]{2,1,0:T(8,128)(2,1)}, u32[]{:S(2)}) %copy-start) | copy-done | bytes 1310744
  1.3 0.0 copy-start.1
  1.3 0.9 %copy-done.1 = bf16[64,10,8,8]{0,3,2,1:T(8,128)(2,1)S(1)} copy-done((bf16[64,10,8,8]{0,3,2,1:T(8,128)(2,1)S(1)}, bf16[64,10,8,8]{0,3,2,1:T(8,128)(2,1)}, u32[]{:S(2)}) %copy-start.1) | copy-done | bytes 81944
  2.2 0.0 copy-start.2
  2.2 0.7 %copy-done.2 = s32[64,10]{0,1:T(8,128)S(1)} copy-done((s32[64,10]{0,1:T(8,128)S(1)}, s32[64,10]{0,1:T(8,128)}, u32[]{:S(2)}) %copy-start.2) | copy-done | bytes 2584
  2.9 0.0 copy-start.3
  2.9 0.7 %copy-done.3 = s32[64,10]{0,1:T(8,128)S(1)} copy-done((s32[64,10]{0,1:T(8,128)S(1)}, s32[64,10]{0,1:T(8,128)}, u32[]{:S(2)}) %copy-start.3) | copy-done | bytes 2584
  3.6 0.0 copy-start.4
  3.6 0.7 %copy-done.4 = s32[64,10]{0,1:T(8,128)S(1)} copy-done((s32[64,10]{0,1:T(8,128)S(1)}, s32[64,10]{0,1:T(8,128)}, u32[]{:S(2)}) %copy-start.4) | copy-done | bytes 2584
  4.3 48.3 %shard_map.55 = f32[16,4096]{1,0:T(8,128)S(1)} custom-call(s32[10,64]{1,0:T(8,128)S(1)} %bitcast.9, s32[10,64]{1,0:T(8,128)S(1)} %bitcast.10, s32[10,64]{1,0:T(8,128)S(1)} %bitcast.11, bf16[10,8,8,64]{3,2,1,0:T(8,128)(2,1)S(1)} %bitcast.8, bf16[160,4096]{1,0:T(8,128)(2,1)S(1)} %bitcast.6), custom_call_target="tpu_custom_call" | custom-call | tf_op jit(solution)/shard_map/pallas_call | solution.py:251
  52.6 0.7 %copy.7 = f32[2,8,4096]{2,1,0:T(8,128)} copy(f32[2,8,4096]{2,1,0:T(8,128)S(1)} %bitcast.7) | data formatting | bytes 524288
Async XLA Ops:
  0.0 1.3 %copy-start = (bf16[20,8,4096]{2,1,0:T(8,128)(2,1)S(1)}, bf16[20,8,4096]{2,1,0:T(8,128)(2,1)}, u32[]{:S(2)}) copy-start(bf16[20,8,4096]{2,1,0:T(8,128)(2,1)} %param.5) | copy-start | bytes 3932164
  1.3 0.9 %copy-start.1 = (bf16[64,10,8,8]{0,3,2,1:T(8,128)(2,1)S(1)}, bf16[64,10,8,8]{0,3,2,1:T(8,128)(2,1)}, u32[]{:S(2)}) copy-start(bf16[64,10,8,8]{0,3,2,1:T(8,128)(2,1)} %param.6) | copy-start | bytes 245764
  2.2 0.7 %copy-start.2 = (s32[64,10]{0,1:T(8,128)S(1)}, s32[64,10]{0,1:T(8,128)}, u32[]{:S(2)}) copy-start(s32[64,10]{0,1:T(8,128)} %param.7) | copy-start | bytes 7684
  2.9 0.7 %copy-start.3 = (s32[64,10]{0,1:T(8,128)S(1)}, s32[64,10]{0,1:T(8,128)}, u32[]{:S(2)}) copy-start(s32[64,10]{0,1:T(8,128)} %param.8) | copy-start | bytes 7684
  3.6 0.7 %copy-start.4 = (s32[64,10]{0,1:T(8,128)S(1)}, s32[64,10]{0,1:T(8,128)}, u32[]{:S(2)}) copy-start(s32[64,10]{0,1:T(8,128)} %param.9) | copy-start | bytes 7684

commit v4 on v3

--- a/solution.py
+++ b/solution.py
@@ -11,12 +11,21 @@
 MESH = pl.DeviceIdType.MESH
 CORES = 2
 TILE = 128
-AXES = ("x", "z", "y")
-
-
-def lay_out(length):
+
+
+def split_z(size):
+    axes, stride = [], 1
+    while size > 1:
+        part = 2 if size % 2 == 0 else size
+        axes.append((f"z{len(axes)}", part, stride))
+        size, stride = size // part, stride * part
+    return axes
+
+
+def lay_out(length, along_z):
+    plane = (("x", "y"), ("y", "x"))
     tiles = length // TILE
-    side = tiles // 8
+    side = tiles * 3 // 16
     widths = []
     left = (tiles - side) // 2
     while left:
@@ -26,9 +35,9 @@
     groups, start = [], 0
     for number, wide in enumerate(widths):
         tasks, at = [], start
-        plan = [("xyz", wide), ("yxz", wide)]
+        plan = [(order + along_z, wide) for order in plane]
         if spare:
-            plan.append((("zxy", "zyx")[number % 2], 1))
+            plan.append((along_z + plane[number % 2], 1))
             spare -= 1
         for order, count in plan:
             tasks.append((order, at * TILE, count * TILE))
@@ -41,12 +50,18 @@
 def repair_kernel(
     sizes,
     groups,
+    rack_hbm,
+    node_hbm,
+    block_hbm,
+    coeffs_hbm,
+    stored_hbm,
+    out_ref,
     rack_ref,
     node_ref,
     block_ref,
     coeffs_ref,
     stored_ref,
-    out_ref,
+    copy_in,
     weights,
     core_send,
     core_recv,
@@ -54,16 +69,20 @@
     task_recv,
     *buffers,
 ):
-    counts, helpers, hold, planes, repairs, per_rack = sizes
+    counts, z_axes, helpers, hold, planes, repairs, per_rack = sizes
     ny = counts["y"]
+    axes = tuple(counts)
     tasks = [task for group in groups for task in group[2]]
     wide, fetched = buffers[: len(groups)], buffers[len(groups) : 2 * len(groups)]
     held = buffers[2 * len(groups) :]
-    held = [held[4 * t : 4 * t + 4] for t in range(len(tasks))]
+    depth = len(axes) + 1
+    held = [held[depth * t : depth * (t + 1)] for t in range(len(tasks))]
 
     rack, node = lax.axis_index("rack"), lax.axis_index("node")
     core = lax.rem(rack, CORES)
-    place = {"x": lax.div(rack, CORES), "z": lax.div(node, ny), "y": lax.rem(node, ny)}
+    place = {"x": lax.div(rack, CORES), "y": lax.rem(node, ny)}
+    for name, size, stride in z_axes:
+        place[name] = lax.rem(lax.div(node, ny * stride), size)
 
     def moved(axis, step):
         return lax.rem(place[axis] + step, counts[axis])
@@ -71,14 +90,29 @@
     def device(axis, step):
         to = dict(place)
         to[axis] = moved(axis, step)
-        return (to["x"] * CORES + core, to["z"] * ny + to["y"])
+        z = sum(to[name] * stride for name, _, stride in z_axes)
+        return (to["x"] * CORES + core, z * ny + to["y"])
 
     other_rack = place["x"] * CORES + lax.rem(core + 1, CORES)
     other_core = (other_rack, node)
-    peers = [other_core] + [device(a, s) for a in AXES for s in range(1, counts[a])]
+    peers = [other_core] + [device(a, s) for a in axes for s in range(1, counts[a])]
     barrier = pltpu.get_barrier_semaphore()
     for peer in peers:
         pl.semaphore_signal(barrier, inc=1, device_id=peer, device_id_type=MESH)
+
+    arrays = (
+        (stored_hbm, stored_ref),
+        (rack_hbm, rack_ref),
+        (node_hbm, node_ref),
+        (block_hbm, block_ref),
+        (coeffs_hbm, coeffs_ref),
+    )
+    loads = [
+        pltpu.make_async_copy(source, target, copy_in.at[i])
+        for i, (source, target) in enumerate(arrays)
+    ]
+    for load in loads:
+        load.start()
 
     def remote(source, target, send, recv, to):
         return pltpu.make_async_remote_copy(
@@ -93,8 +127,11 @@
     def core_copy(g):
         return remote(wide[g], fetched[g], core_send.at[g], core_recv.at[g], other_core)
 
+    loads[0].wait()
     for g, (start, width, _) in enumerate(groups):
         wide[g][...] = stored_ref[:, start : start + width].astype(jnp.float32)
+    for load in loads[1:]:
+        load.wait()
 
     here = node_ref[...] == node
     marks = jnp.where(
@@ -135,7 +172,7 @@
 
     def before(t, stage):
         order = tasks[t][0]
-        left = [axis for axis in AXES if axis not in order[:stage]]
+        left = [axis for axis in axes if axis not in order[:stage]]
         ahead = (slice(None),) * left.index(order[stage])
         if stage == 0:
             return held[t][0], lambda at: ahead + (at,)
@@ -189,7 +226,7 @@
     def finish(g):
         for t in members[g]:
             _, at, count = tasks[t]
-            out_ref[:, at : at + count] = gathered(t, len(AXES) - 1)
+            out_ref[:, at : at + count] = gathered(t, len(axes) - 1)
 
     members, seen = [], 0
     for _, _, inside in groups:
@@ -197,11 +234,10 @@
         seen += len(inside)
     steps = (
         begin,
-        functools.partial(advance, stage=1),
-        functools.partial(advance, stage=2),
+        *[functools.partial(advance, stage=stage) for stage in range(1, len(axes))],
         finish,
     )
-    delays = (0, 1, 2, 6)
+    delays = (*range(len(axes)), len(axes) + 3)
     for tick in range(len(groups) + delays[-1]):
         for delay, step in zip(delays, steps):
             if 0 <= tick - delay < len(groups):
@@ -210,36 +246,39 @@
     for g in range(len(groups)):
         core_copy(g).wait_send()
         for t in members[g]:
-            for stage in range(len(AXES)):
+            for stage in range(len(axes)):
                 for copy in copies(t, stage):
                     copy.wait_send()
 
 
 def solution(mesh):
     racks, nodes = mesh.shape["rack"], mesh.shape["node"]
-    counts = {"x": racks // CORES, "y": 2, "z": nodes // 2}
+    z_axes = split_z(nodes // 2)
+    counts = {"x": racks // CORES}
+    counts.update({name: size for name, size, _ in reversed(z_axes)})
+    counts["y"] = 2
 
     def on_device(stored, coefficients, helper_rack, helper_node, helper_block):
         hold, planes, length = stored.shape
         repairs, helpers = helper_block.shape
         out_rows = repairs // (racks * nodes) * planes
-        groups = lay_out(length)
+        groups = lay_out(length, tuple(name for name, _, _ in z_axes))
         tasks = [task for group in groups for task in group[2]]
-        sizes = (counts, helpers, hold, planes, repairs, repairs // racks)
+        sizes = (counts, z_axes, helpers, hold, planes, repairs, repairs // racks)
         buffers = [
             pltpu.VMEM((hold * planes, width), jnp.float32)
             for _ in range(2)
             for _, width, _ in groups
         ]
         for order, _, width in tasks:
-            for stage in range(len(AXES) + 1):
-                left = [counts[a] for a in AXES if a not in order[:stage]]
+            for stage in range(len(counts) + 1):
+                left = [counts[a] for a in counts if a not in order[:stage]]
                 if stage:
                     left = [counts[order[stage - 1]] - 1] + left
                 buffers.append(pltpu.VMEM((*left, out_rows, width), jnp.float32))
         most = max(counts.values()) - 1
         dma = pltpu.SemaphoreType.DMA
-        vmem = pl.BlockSpec(memory_space=pltpu.VMEM)
+        hbm = pl.BlockSpec(memory_space=pltpu.HBM)
         operands = (
             helper_rack.T,
             helper_node.T,
@@ -251,20 +290,22 @@
         rebuilt = pl.pallas_call(
             functools.partial(repair_kernel, sizes, groups),
             out_shape=jax.ShapeDtypeStruct((out_rows, length), jnp.float32),
-            in_specs=[vmem] * len(operands),
-            out_specs=vmem,
+            in_specs=[hbm] * 5,
+            out_specs=pl.BlockSpec(memory_space=pltpu.VMEM),
             scratch_shapes=[
+                *[pltpu.VMEM(a.shape, a.dtype) for a in operands],
+                dma((len(operands),)),
                 pltpu.VMEM((2, repairs * planes // CORES, hold * planes), jnp.bfloat16),
                 dma((len(groups),)),
                 dma((len(groups),)),
-                dma((len(tasks), len(AXES), most)),
-                dma((len(tasks), len(AXES), most)),
+                dma((len(tasks), len(counts), most)),
+                dma((len(tasks), len(counts), most)),
                 *buffers,
             ],
             compiler_params=pltpu.CompilerParams(
                 collective_id=0,
                 has_side_effects=True,
-                vmem_limit_bytes=buffer_bytes + 12 * 1024 * 1024,
+                vmem_limit_bytes=max(buffer_bytes + 12 * 2**20, 56 * 2**20),
             ),
         )(*operands)
         return rebuilt.reshape(-1, planes, length)

time: 53.7 us -> 49.7 us (0.926)
  local copies, waits for them, and re-layouts: 5.03 us -> 1.67 us
    unnamed x11 -> x1, local copies, waits for them, and re-layouts: 5.03 us -> 1.67 us
where the time goes in v4:
time: 49.7 us; the launch traced here: 49.6 us
  Pallas kernels  47.9 us (96%)
  local copies, waits for them, and re-layouts  1.67 us (3%)
    pallas_call x1, Pallas kernels, on_device(): pl.pallas_call(functools.partial(repair_kernel, sizes, groups), out_shape...  47.9 us
    unnamed x1, local copies, waits for them, and re-layouts  1.67 us

profile of v4, /device:TPU:0, one launch (start us, length us, event | category | flops | bytes accessed | tf_op | source)
XLA Modules:
  0.0 49.6 jit_solution(18213284317053913442)
XLA Ops:
  0.0 47.9 %shard_map.55 = f32[16,4096]{1,0:T(8,128)} custom-call(s32[10,64]{1,0:T(8,128)} %bitcast.9, s32[10,64]{1,0:T(8,128)} %bitcast.10, s32[10,64]{1,0:T(8,128)} %bitcast.11, bf16[10,8,8,64]{3,2,1,0:T(8,128)(2,1)} %bitcast.8, bf16[160,4096]{1,0:T(8,128)(2,1)} %bitcast.6), custom_call_target="tpu_custom_call" | custom-call | tf_op jit(solution)/shard_map/pallas_call | solution.py:290
  47.9 1.7 %copy.7 = f32[2,8,4096]{2,1,0:T(8,128)} copy(f32[2,8,4096]{2,1,0:T(8,128)} %bitcast.7) | data formatting | bytes 524288

commit v5 on v4

--- a/solution.py
+++ b/solution.py
@@ -26,10 +26,10 @@
     plane = (("x", "y"), ("y", "x"))
     tiles = length // TILE
     side = tiles * 3 // 16
-    widths = []
-    left = (tiles - side) // 2
+    widths = [1]
+    left = (tiles - side) // 2 - 1
     while left:
-        widths.append(2 if left > 2 else 1)
+        widths.append(2 if left > 3 else 1)
         left -= widths[-1]
     spare = tiles - 2 * sum(widths)
     groups, start = [], 0
@@ -55,7 +55,8 @@
     block_hbm,
     coeffs_hbm,
     stored_hbm,
-    out_ref,
+    own_ref,
+    came_ref,
     rack_ref,
     node_ref,
     block_ref,
@@ -101,11 +102,11 @@
         pl.semaphore_signal(barrier, inc=1, device_id=peer, device_id_type=MESH)
 
     arrays = (
-        (stored_hbm, stored_ref),
         (rack_hbm, rack_ref),
         (node_hbm, node_ref),
         (block_hbm, block_ref),
         (coeffs_hbm, coeffs_ref),
+        (stored_hbm, stored_ref),
     )
     loads = [
         pltpu.make_async_copy(source, target, copy_in.at[i])
@@ -127,10 +128,7 @@
     def core_copy(g):
         return remote(wide[g], fetched[g], core_send.at[g], core_recv.at[g], other_core)
 
-    loads[0].wait()
-    for g, (start, width, _) in enumerate(groups):
-        wide[g][...] = stored_ref[:, start : start + width].astype(jnp.float32)
-    for load in loads[1:]:
+    for load in loads[:-1]:
         load.wait()
 
     here = node_ref[...] == node
@@ -140,26 +138,37 @@
         jnp.where(here & (rack_ref[...] == other_rack), block_ref[...] + hold, -1),
     )
     own_rows = repairs * planes // CORES
-    row = lax.broadcasted_iota(jnp.int32, (own_rows, repairs), 0)
+    row = lax.broadcasted_iota(jnp.int32, (own_rows, 2 * repairs), 0)
+    column = lax.broadcasted_iota(jnp.int32, (own_rows, 2 * repairs), 1)
     row_plane, row_repair = lax.rem(row, planes), lax.div(row, planes)
     row_repair = (
         lax.div(row_repair, per_rack) * CORES + core
     ) * per_rack + lax.rem(row_repair, per_rack)
-    hits = row_repair == lax.broadcasted_iota(jnp.int32, (own_rows, repairs), 1)
-    slot = lax.broadcasted_iota(jnp.int32, (2 * hold, planes, repairs), 0)
+    hits = row_repair == lax.rem(column, repairs)
+    half = planes // 2
+    hit_plane = row_plane - lax.div(column, repairs) * half
+    marks = jnp.concatenate([marks, marks], axis=1)
+    slot = lax.broadcasted_iota(jnp.int32, (2 * hold, planes, 2 * repairs), 0)
     summed = [jnp.zeros((own_rows, hold * planes), jnp.float32)] * 2
-    for plane in range(planes):
-        if plane == planes // 2:
+    for plane in range(half):
+        if plane == half // 2:
+            loads[-1].wait()
+            for g, (start, width, _) in enumerate(groups):
+                piece = stored_ref[:, start : start + width]
+                wide[g][...] = piece.astype(jnp.float32)
             pl.semaphore_wait(barrier, len(peers))
             for g in range(len(groups)):
                 core_copy(g).start()
-        spread = jnp.zeros((2 * hold, planes, repairs), jnp.float32)
+        spread = jnp.zeros((2 * hold, planes, 2 * repairs), jnp.float32)
         for helper in range(helpers):
-            values = coeffs_ref[helper, plane].astype(jnp.float32)[None]
+            values = [coeffs_ref[helper, plane + k * half] for k in range(2)]
+            values = [value.astype(jnp.float32) for value in values]
             mark = marks[helper : helper + 1, :][None]
-            spread = jnp.where(slot == mark, values, spread)
-        spread = spread.reshape(2 * hold * planes, repairs).astype(jnp.bfloat16)
-        picked = (hits & (row_plane == plane)).astype(jnp.float32).astype(jnp.bfloat16)
+            spread = jnp.where(
+                slot == mark, jnp.concatenate(values, axis=1)[None], spread
+            )
+        spread = spread.reshape(2 * hold * planes, 2 * repairs).astype(jnp.bfloat16)
+        picked = (hits & (hit_plane == plane)).astype(jnp.float32).astype(jnp.bfloat16)
         for part in range(2):
             summed[part] += lax.dot_general(
                 picked,
@@ -198,10 +207,10 @@
         arrived = copies(t, stage)
         for copy in arrived:
             copy.wait_recv()
-        total = source[pick(place[axis])]
-        for s in range(len(arrived)):
-            total += held[t][stage + 1][s]
-        return total
+        came = held[t][stage + 1][0]
+        for s in range(1, len(arrived)):
+            came += held[t][stage + 1][s]
+        return source[pick(place[axis])], came
 
     def begin(g):
         start, width, inside = groups[g]
@@ -219,14 +228,17 @@
 
     def advance(g, stage):
         for t in members[g]:
-            held[t][stage][0] = gathered(t, stage - 1)
+            own, came = gathered(t, stage - 1)
+            held[t][stage][0] = own + came
             for copy in copies(t, stage):
                 copy.start()
 
     def finish(g):
         for t in members[g]:
             _, at, count = tasks[t]
-            out_ref[:, at : at + count] = gathered(t, len(axes) - 1)
+            own, came = gathered(t, len(axes) - 1)
+            own_ref[:, at : at + count] = own
+            came_ref[:, at : at + count] = came
 
     members, seen = [], 0
     for _, _, inside in groups:
@@ -287,11 +299,11 @@
             stored.reshape(hold * planes, length),
         )
         buffer_bytes = sum(math.prod(b.shape) * 4 for b in buffers)
-        rebuilt = pl.pallas_call(
+        own, came = pl.pallas_call(
             functools.partial(repair_kernel, sizes, groups),
-            out_shape=jax.ShapeDtypeStruct((out_rows, length), jnp.float32),
+            out_shape=[jax.ShapeDtypeStruct((out_rows, length), jnp.float32)] * 2,
             in_specs=[hbm] * 5,
-            out_specs=pl.BlockSpec(memory_space=pltpu.VMEM),
+            out_specs=[pl.BlockSpec(memory_space=pltpu.VMEM)] * 2,
             scratch_shapes=[
                 *[pltpu.VMEM(a.shape, a.dtype) for a in operands],
                 dma((len(operands),)),
@@ -308,7 +320,7 @@
                 vmem_limit_bytes=max(buffer_bytes + 12 * 2**20, 56 * 2**20),
             ),
         )(*operands)
-        return rebuilt.reshape(-1, planes, length)
+        return (own + came).reshape(-1, planes, length)
 
     return jax.shard_map(
         on_device,

time: 49.7 us -> 50.5 us (1.016)
  other arithmetic: 0 us -> 1.76 us
  local copies, waits for them, and re-layouts: 1.67 us -> 0 us
  Pallas kernels: 47.9 us -> 48.6 us
    reshape x0 -> x1, other arithmetic: none -> 1.76 us  [on_device(): return (own + came).reshape(-1, planes, length)]
    unnamed x1 -> x0, local copies, waits for them, and re-layouts: 1.67 us -> none
    pallas_call x1, Pallas kernels: 47.9 us -> 48.6 us  [on_device(): pl.pallas_call(functools.partial(repair_kernel, sizes, groups), out_shape...]
where the time goes in v5:
time: 50.5 us; the launch traced here: 50.3 us
  Pallas kernels  48.6 us (96%)
  other arithmetic  1.76 us (3%)
    pallas_call x1, Pallas kernels, on_device(): pl.pallas_call(functools.partial(repair_kernel, sizes, groups), out_shape...  48.6 us
    reshape x1, other arithmetic, on_device(): return (own + came).reshape(-1, planes, length)  1.76 us

profile of v5, /device:TPU:0, one launch (start us, length us, event | category | flops | bytes accessed | tf_op | source)
XLA Modules:
  0.0 50.3 jit_solution(7721692927421959168)
XLA Ops:
  0.0 48.6 %shard_map.55 = (f32[16,4096]{1,0:T(8,128)}, f32[16,4096]{1,0:T(8,128)}) custom-call(s32[10,64]{1,0:T(8,128)} %bitcast.9, s32[10,64]{1,0:T(8,128)} %bitcast.10, s32[10,64]{1,0:T(8,128)} %bitcast.11, bf16[10,8,8,64]{3,2,1,0:T(8,128)(2,1)} %bitcast.8, bf16[160,4096]{1,0:T(8,128)(2,1)} %bitcast.7), custom_call_target="tpu_custom_call" | custom-call | tf_op jit(solution)/shard_map/pallas_call | solution.py:302
  48.6 1.8 %add_bitcast_fusion = f32[2,8,4096]{2,1,0:T(8,128)} fusion(f32[16,4096]{1,0:T(8,128)} %get-tuple-element.7, f32[16,4096]{1,0:T(8,128)} %get-tuple-element.8), kind=kLoop, calls=%fused_computation | loop fusion | flops 65536 | bytes 786432 | tf_op jit(solution)/shard_map/reshape | solution.py:323

commit v6 on v5

--- a/solution.py
+++ b/solution.py
@@ -26,10 +26,10 @@
     plane = (("x", "y"), ("y", "x"))
     tiles = length // TILE
     side = tiles * 3 // 16
-    widths = [1]
-    left = (tiles - side) // 2 - 1
+    widths = []
+    left = (tiles - side) // 2
     while left:
-        widths.append(2 if left > 3 else 1)
+        widths.append(min(2, left))
         left -= widths[-1]
     spare = tiles - 2 * sum(widths)
     groups, start = [], 0
@@ -37,8 +37,9 @@
         tasks, at = [], start
         plan = [(order + along_z, wide) for order in plane]
         if spare:
-            plan.append((along_z + plane[number % 2], 1))
-            spare -= 1
+            part = 2 if spare > 2 else 1
+            plan.append((along_z + plane[number % 2], part))
+            spare -= part
         for order, count in plan:
             tasks.append((order, at * TILE, count * TILE))
             at += count
@@ -55,8 +56,7 @@
     block_hbm,
     coeffs_hbm,
     stored_hbm,
-    own_ref,
-    came_ref,
+    out_ref,
     rack_ref,
     node_ref,
     block_ref,
@@ -237,8 +237,7 @@
         for t in members[g]:
             _, at, count = tasks[t]
             own, came = gathered(t, len(axes) - 1)
-            own_ref[:, at : at + count] = own
-            came_ref[:, at : at + count] = came
+            out_ref[:, at : at + count] = own + came
 
     members, seen = [], 0
     for _, _, inside in groups:
@@ -249,7 +248,7 @@
         *[functools.partial(advance, stage=stage) for stage in range(1, len(axes))],
         finish,
     )
-    delays = (*range(len(axes)), len(axes) + 3)
+    delays = (0, *range(2, len(axes) + 1), len(axes) + 4)
     for tick in range(len(groups) + delays[-1]):
         for delay, step in zip(delays, steps):
             if 0 <= tick - delay < len(groups):
@@ -299,11 +298,11 @@
             stored.reshape(hold * planes, length),
         )
         buffer_bytes = sum(math.prod(b.shape) * 4 for b in buffers)
-        own, came = pl.pallas_call(
+        rebuilt = pl.pallas_call(
             functools.partial(repair_kernel, sizes, groups),
-            out_shape=[jax.ShapeDtypeStruct((out_rows, length), jnp.float32)] * 2,
+            out_shape=jax.ShapeDtypeStruct((out_rows, length), jnp.float32),
             in_specs=[hbm] * 5,
-            out_specs=[pl.BlockSpec(memory_space=pltpu.VMEM)] * 2,
+            out_specs=pl.BlockSpec(memory_space=pltpu.VMEM),
             scratch_shapes=[
                 *[pltpu.VMEM(a.shape, a.dtype) for a in operands],
                 dma((len(operands),)),
@@ -320,7 +319,7 @@
                 vmem_limit_bytes=max(buffer_bytes + 12 * 2**20, 56 * 2**20),
             ),
         )(*operands)
-        return (own + came).reshape(-1, planes, length)
+        return rebuilt.reshape(-1, planes, length)
 
     return jax.shard_map(
         on_device,

time: 50.5 us -> 50.2 us (level)
  other arithmetic: 1.76 us -> 0 us
  local copies, waits for them, and re-layouts: 0 us -> 1.67 us
    reshape x1 -> x0, other arithmetic: 1.76 us -> none  [on_device(): return (own + came).reshape(-1, planes, length)]
    unnamed x0 -> x1, local copies, waits for them, and re-layouts: none -> 1.67 us
where the time goes in v6:
time: 50.2 us; the launch traced here: 50 us
  Pallas kernels  48.3 us (96%)
  local copies, waits for them, and re-layouts  1.67 us (3%)
    pallas_call x1, Pallas kernels, on_device(): pl.pallas_call(functools.partial(repair_kernel, sizes, groups), out_shape...  48.3 us
    unnamed x1, local copies, waits for them, and re-layouts  1.67 us

profile of v6, /device:TPU:0, one launch (start us, length us, event | category | flops | bytes accessed | tf_op | source)
XLA Modules:
  0.0 50.0 jit_solution(1025519344215229951)
XLA Ops:
  0.0 48.3 %shard_map.55 = f32[16,4096]{1,0:T(8,128)} custom-call(s32[10,64]{1,0:T(8,128)} %bitcast.9, s32[10,64]{1,0:T(8,128)} %bitcast.10, s32[10,64]{1,0:T(8,128)} %bitcast.11, bf16[10,8,8,64]{3,2,1,0:T(8,128)(2,1)} %bitcast.8, bf16[160,4096]{1,0:T(8,128)(2,1)} %bitcast.6), custom_call_target="tpu_custom_call" | custom-call | tf_op jit(solution)/shard_map/pallas_call | solution.py:301
  48.3 1.7 %copy.7 = f32[2,8,4096]{2,1,0:T(8,128)} copy(f32[2,8,4096]{2,1,0:T(8,128)} %bitcast.7) | data formatting | bytes 524288

commit v7 on v6

--- a/solution.py
+++ b/solution.py
@@ -25,7 +25,7 @@
 def lay_out(length, along_z):
     plane = (("x", "y"), ("y", "x"))
     tiles = length // TILE
-    side = tiles * 3 // 16
+    side = tiles // 4
     widths = []
     left = (tiles - side) // 2
     while left:
@@ -37,7 +37,7 @@
         tasks, at = [], start
         plan = [(order + along_z, wide) for order in plane]
         if spare:
-            part = 2 if spare > 2 else 1
+            part = -(-spare // (len(widths) - number))
             plan.append((along_z + plane[number % 2], part))
             spare -= part
         for order, count in plan:
@@ -248,7 +248,7 @@
         *[functools.partial(advance, stage=stage) for stage in range(1, len(axes))],
         finish,
     )
-    delays = (0, *range(2, len(axes) + 1), len(axes) + 4)
+    delays = (*range(len(axes)), len(axes) + 3)
     for tick in range(len(groups) + delays[-1]):
         for delay, step in zip(delays, steps):
             if 0 <= tick - delay < len(groups):

time: 50.2 us -> 48 us (0.956)
  Pallas kernels: 48.3 us -> 46.1 us
    pallas_call x1, Pallas kernels: 48.3 us -> 46.1 us  [on_device(): pl.pallas_call(functools.partial(repair_kernel, sizes, groups), out_shape...]
where the time goes in v7:
time: 48 us; the launch traced here: 47.8 us
  Pallas kernels  46.1 us (96%)
  local copies, waits for them, and re-layouts  1.67 us (3%)
    pallas_call x1, Pallas kernels, on_device(): pl.pallas_call(functools.partial(repair_kernel, sizes, groups), out_shape...  46.1 us
    unnamed x1, local copies, waits for them, and re-layouts  1.67 us

profile of v7, /device:TPU:0, one launch (start us, length us, event | category | flops | bytes accessed | tf_op | source)
XLA Modules:
  0.0 47.8 jit_solution(13651623480588811060)
XLA Ops:
  0.0 46.1 %shard_map.55 = f32[16,4096]{1,0:T(8,128)} custom-call(s32[10,64]{1,0:T(8,128)} %bitcast.9, s32[10,64]{1,0:T(8,128)} %bitcast.10, s32[10,64]{1,0:T(8,128)} %bitcast.11, bf16[10,8,8,64]{3,2,1,0:T(8,128)(2,1)} %bitcast.8, bf16[160,4096]{1,0:T(8,128)(2,1)} %bitcast.6), custom_call_target="tpu_custom_call" | custom-call | tf_op jit(solution)/shard_map/pallas_call | solution.py:301
  46.1 1.7 %copy.7 = f32[2,8,4096]{2,1,0:T(8,128)} copy(f32[2,8,4096]{2,1,0:T(8,128)} %bitcast.7) | data formatting | bytes 524288

commit v8 on v7

--- a/solution.py
+++ b/solution.py
@@ -25,7 +25,7 @@
 def lay_out(length, along_z):
     plane = (("x", "y"), ("y", "x"))
     tiles = length // TILE
-    side = tiles // 4
+    side = tiles * 3 // 8
     widths = []
     left = (tiles - side) // 2
     while left:

time: 48 us -> 52.4 us (1.092)
  Pallas kernels: 46.1 us -> 50.5 us
    pallas_call x1, Pallas kernels: 46.1 us -> 50.5 us  [on_device(): pl.pallas_call(functools.partial(repair_kernel, sizes, groups), out_shape...]
where the time goes in v8:
time: 52.4 us; the launch traced here: 52.2 us
  Pallas kernels  50.5 us (96%)
  local copies, waits for them, and re-layouts  1.67 us (3%)
    pallas_call x1, Pallas kernels, on_device(): pl.pallas_call(functools.partial(repair_kernel, sizes, groups), out_shape...  50.5 us
    unnamed x1, local copies, waits for them, and re-layouts  1.67 us

profile of v8, /device:TPU:0, one launch (start us, length us, event | category | flops | bytes accessed | tf_op | source)
XLA Modules:
  0.0 52.2 jit_solution(13896772638824052886)
XLA Ops:
  0.0 50.5 %shard_map.55 = f32[16,4096]{1,0:T(8,128)} custom-call(s32[10,64]{1,0:T(8,128)} %bitcast.9, s32[10,64]{1,0:T(8,128)} %bitcast.10, s32[10,64]{1,0:T(8,128)} %bitcast.11, bf16[10,8,8,64]{3,2,1,0:T(8,128)(2,1)} %bitcast.8, bf16[160,4096]{1,0:T(8,128)(2,1)} %bitcast.6), custom_call_target="tpu_custom_call" | custom-call | tf_op jit(solution)/shard_map/pallas_call | solution.py:301
  50.6 1.7 %copy.7 = f32[2,8,4096]{2,1,0:T(8,128)} copy(f32[2,8,4096]{2,1,0:T(8,128)} %bitcast.7) | data formatting | bytes 524288

commit v9 on v7

--- a/solution.py
+++ b/solution.py
@@ -37,7 +37,7 @@
         tasks, at = [], start
         plan = [(order + along_z, wide) for order in plane]
         if spare:
-            part = -(-spare // (len(widths) - number))
+            part = min(2, spare)
             plan.append((along_z + plane[number % 2], part))
             spare -= part
         for order, count in plan:

time: 48 us -> 49.1 us (1.023)
  Pallas kernels: 46.1 us -> 47.3 us
    pallas_call x1, Pallas kernels: 46.1 us -> 47.3 us  [on_device(): pl.pallas_call(functools.partial(repair_kernel, sizes, groups), out_shape...]
where the time goes in v9:
time: 49.1 us; the launch traced here: 48.9 us
  Pallas kernels  47.3 us (96%)
  local copies, waits for them, and re-layouts  1.67 us (3%)
    pallas_call x1, Pallas kernels, on_device(): pl.pallas_call(functools.partial(repair_kernel, sizes, groups), out_shape...  47.3 us
    unnamed x1, local copies, waits for them, and re-layouts  1.67 us

profile of v9, /device:TPU:0, one launch (start us, length us, event | category | flops | bytes accessed | tf_op | source)
XLA Modules:
  0.0 48.9 jit_solution(6326554346336667234)
XLA Ops:
  0.0 47.3 %shard_map.55 = f32[16,4096]{1,0:T(8,128)} custom-call(s32[10,64]{1,0:T(8,128)} %bitcast.9, s32[10,64]{1,0:T(8,128)} %bitcast.10, s32[10,64]{1,0:T(8,128)} %bitcast.11, bf16[10,8,8,64]{3,2,1,0:T(8,128)(2,1)} %bitcast.8, bf16[160,4096]{1,0:T(8,128)(2,1)} %bitcast.6), custom_call_target="tpu_custom_call" | custom-call | tf_op jit(solution)/shard_map/pallas_call | solution.py:301
  47.3 1.7 %copy.7 = f32[2,8,4096]{2,1,0:T(8,128)} copy(f32[2,8,4096]{2,1,0:T(8,128)} %bitcast.7) | data formatting | bytes 524288
